TPU v7x, 128 devices: a whole 4x4x4 slice. The times are simulated.
128 devices in a mesh: wide: 16 (over z_hi, x, core), narrow: 8 (over z_lo, y).
Axes of the slice: x: 4, y: 4, z: 4 (z_hi: 2, z_lo: 2; z = z_hi * 2 + z_lo), core: 2. Of those that a mesh axis runs over, the one named last changes fastest.
Arguments:
- root_front: float32 [6, 16, 128, 12, 8, 128], P(None, 'wide', None, None, 'narrow'), may hold values from -1 to 67.88225, as said below
- child_update: float32 [16, 3, 16, 64, 12, 8, 64], P('wide', None, None, None, None, 'narrow'), may hold values from -0.5 to 1.5, as said below
- child_map: int32 [8, 6144], replicated, may hold values from 0 to 12287, as said below
Outputs:
- factored: float32 [6, 16, 128, 12, 8, 128], P(None, 'wide', None, None, 'narrow')
Inputs may be any that keep to these rules, and one draw needn't show every extreme that they name: `child_map`: row g lists 6144 distinct root indices in increasing order, exactly 64 of them in each aligned block of 128 root indices; rows 2h and 2h + 1 together hold every root index once. Read as a matrix, root_front is symmetric with a positive diagonal larger than its other entries. `child_update`: each S_g is symmetric with a positive diagonal.
All inputs are finite; a program needn't handle non-finite values.
Results may differ from a plain program's by a relative error of at most 0.0001.
Values sent between devices are 32-bit elements; how exact they have to be, the bound alone decides.
A program may use at most 192 MiB of HBM per device.

v0:
```python
import jax
import jax.numpy as jnp
from jax import lax
from jax.sharding import PartitionSpec as P

ROOT = 12288
BLOCK = 128
PANEL = 256
PANELS = 2
HALF = 64


def spread_2(value, axis, source):
    kept = jnp.where(lax.axis_index(axis) == source, value, 0).astype(value.dtype)
    return lax.psum(kept, axis)


def one_hot_table(positions, table_width):
    levels = jnp.arange(table_width, dtype=jnp.int32)
    return (positions[..., None, :] == levels[:, None]).astype(jnp.float32)


def body(root_front, child_update, child_map):
    wide_count = lax.axis_size("wide")
    narrow_count = lax.axis_size("narrow")
    wide_index = lax.axis_index("wide")
    narrow_index = lax.axis_index("narrow")
    groups = child_map.shape[0]
    blocks_all = ROOT // BLOCK
    sub_count = wide_count // groups
    row_blocks = blocks_all // wide_count
    col_blocks = blocks_all // narrow_count
    pair_blocks = row_blocks // sub_count
    front_now = root_front.reshape(row_blocks, BLOCK, col_blocks, BLOCK)
    pieces = child_update.reshape(pair_blocks, wide_count, HALF, col_blocks * HALF)
    arrived = lax.all_to_all(pieces, "wide", split_axis=1, concat_axis=1, tiled=True)
    arrived = arrived.reshape(pair_blocks, wide_count, HALF, col_blocks, HALF)
    starts = (jnp.arange(blocks_all, dtype=jnp.int32) * BLOCK)[None, :, None]
    offsets = child_map.reshape(groups, blocks_all, HALF) - starts
    row_offsets = lax.dynamic_index_in_dim(
        offsets.reshape(groups, row_blocks, wide_count, HALF), wide_index, 2, keepdims=False
    )
    row_offsets = (
        row_offsets.reshape(groups, pair_blocks, sub_count, HALF)
        .transpose(0, 2, 1, 3)
        .reshape(wide_count, pair_blocks, HALF)
    )
    col_offsets = lax.dynamic_index_in_dim(
        offsets.reshape(groups, col_blocks, narrow_count, HALF), narrow_index, 2, keepdims=False
    )
    row_table = one_hot_table(row_offsets, BLOCK)
    col_table = one_hot_table(col_offsets, BLOCK)
    spread = jnp.einsum("wkxr,kwrlc->wkxlc", row_table, arrived, precision=lax.Precision.HIGHEST)
    spread = spread.reshape(groups, sub_count, pair_blocks, BLOCK, col_blocks, HALF)
    summed = jnp.einsum("gskxlc,glyc->ksxly", spread, col_table, precision=lax.Precision.HIGHEST)
    front_now = front_now + summed.reshape(row_blocks, BLOCK, col_blocks, BLOCK)
    row_global = (
        jnp.arange(row_blocks, dtype=jnp.int32)[:, None] * wide_count + wide_index
    ) * BLOCK + jnp.arange(BLOCK, dtype=jnp.int32)[None, :]
    col_global = (
        jnp.arange(col_blocks, dtype=jnp.int32)[:, None] * narrow_count + narrow_index
    ) * BLOCK + jnp.arange(BLOCK, dtype=jnp.int32)[None, :]
    per_panel = PANEL // BLOCK
    index_cols = jnp.arange(PANEL, dtype=jnp.int32)
    lower_parts = []
    upper_parts = []
    for panel_step in range(PANELS):
        first_col = panel_step * PANEL
        owned_parts = []
        for member in range(per_panel):
            block_id = panel_step * per_panel + member
            owned_parts.append(
                spread_2(
                    front_now[:, :, block_id // narrow_count, :], "narrow", block_id % narrow_count
                )
            )
        panel_cols = jnp.concatenate(owned_parts, axis=2)
        rows_diag = []
        for member in range(per_panel):
            block_id = panel_step * per_panel + member
            rows_diag.append(
                spread_2(panel_cols[block_id // wide_count], "wide", block_id % wide_count)
            )
        diagonal = jnp.concatenate(rows_diag, axis=0)
        factor = jnp.linalg.cholesky(diagonal)
        solved = lax.linalg.triangular_solve(
            factor,
            panel_cols.reshape(row_blocks * BLOCK, PANEL),
            left_side=False,
            lower=True,
            transpose_a=True,
        )
        keep_mask = row_global.reshape(-1, 1) - first_col >= index_cols[None, :]
        rows_factor = jnp.where(keep_mask, solved, 0.0).reshape(row_blocks, BLOCK, PANEL)
        gathered = lax.all_gather(rows_factor[:, None], "wide", axis=1, tiled=True)
        ordered = gathered.reshape(col_blocks, narrow_count, BLOCK, PANEL)
        cols_factor = lax.dynamic_index_in_dim(ordered, narrow_index, 1, keepdims=False)
        past_col = first_col + PANEL
        row_part = jnp.where((row_global >= past_col)[:, :, None], rows_factor, 0.0)
        col_part = jnp.where((col_global >= past_col)[:, :, None], cols_factor, 0.0)
        front_now = front_now - jnp.einsum(
            "axp,lyp->axly", row_part, col_part, precision=lax.Precision.HIGHEST
        )
        lower_parts.append(rows_factor)
        upper_parts.append(cols_factor)
    span_cols = PANELS * PANEL
    blocks_used = span_cols // BLOCK
    lower_all = jnp.concatenate(lower_parts, axis=2)
    upper_all = jnp.concatenate(upper_parts, axis=2)
    lower_pick = lax.dynamic_slice_in_dim(
        lower_all, jnp.minimum(narrow_index, blocks_used - 1) * BLOCK, BLOCK, 2
    )
    first_cols = col_global[0]
    lower_mask = (row_global[:, :, None] >= first_cols[None, None, :]) & (first_cols < span_cols)[
        None, None, :
    ]
    result = front_now.at[:, :, 0, :].set(jnp.where(lower_mask, lower_pick, front_now[:, :, 0, :]))
    upper_pick = lax.dynamic_slice_in_dim(
        upper_all, jnp.minimum(wide_index, blocks_used - 1) * BLOCK, BLOCK, 2
    )
    upper_pick = upper_pick.transpose(2, 0, 1)
    first_rows = row_global[0]
    upper_mask = (first_rows[:, None, None] < col_global[None, :, :]) & (first_rows < span_cols)[
        :, None, None
    ]
    result = result.at[0].set(jnp.where(upper_mask, upper_pick, result[0]))
    return result.reshape(root_front.shape)


def solution(mesh):
    return jax.shard_map(
        body,
        mesh=mesh,
        in_specs=(
            P(None, "wide", None, None, "narrow", None),
            P("wide", None, None, None, None, "narrow", None),
            P(),
        ),
        out_specs=P(None, "wide", None, None, "narrow", None),
        check_vma=False,
    )
```

profile of v0, /device:TPU:85, one launch (start us, length us, event | category | flops | bytes accessed | tf_op | source)
XLA Modules:
  0.0 1185.2 jit_solution(1486096728546323171)
XLA Ops:
  6.5 166.7 %reduce.12 = f32[3,16,64,12,64]{4,3,2,1,0:T(8,128)} reduce(f32[1,3,16,64,12,1,64]{6,5,4,3,2,1,0:T(1,128)} %param.11, f32[]{:T(128)} %constant.187), dimensions={0,5}, to_apply=%param.11.reduce_sub_computation | reduce | bytes 18874372 | tf_op args[1]
  173.3 19.0 %reshape.356 = f32[3,16,64,768]{3,2,1,0:T(8,128)} reshape(f32[3,16,64,12,64]{4,3,2,1,0:T(8,128)} %reduce.12) | data formatting | bytes 18874368 | tf_op jit(solution)/shard_map/reshape | solution.py:35
  192.3 8.4 copy.96
  200.7 7.7 all-to-all-start
  209.8 12.1 %copy.91 = f32[6,1,128,12,1,128]{2,5,0,3,4,1:T(8,128)} copy(f32[6,1,128,12,1,128]{5,4,3,2,1,0:T(1,128)} %param.10) | data formatting | bytes 9437184 | tf_op args[0]
  221.9 112.2 %all-to-all-done = f32[3,16,64,768]{3,2,0,1:T(8,128)} async-done(((f32[3,16,64,768]{3,2,0,1:T(8,128)}), f32[3,16,64,768]{3,2,0,1:T(8,128)}, u32[]{:S(2)}, u32[]{:S(2)}) %all-to-all-start) | async-done | bytes 9437216 | tf_op jit(solution)/shard_map/all_to_all | solution.py:36
  334.1 13.9 %copy.97 = f32[3,16,64,768]{2,3,0,1:T(8,128)} copy(f32[3,16,64,768]{3,2,0,1:T(8,128)} %all-to-all-done) | data formatting | bytes 18874368 | tf_op jit(solution)/shard_map/all_to_all | solution.py:36
  348.0 13.4 %fusion = f32[16,3,128,768]{2,3,1,0:S(1)} fusion(f32[3,16,64,768]{2,3,0,1:T(8,128)} %copy.97, s32[16,3,64]{2,1,0:T(4,128)S(1)} %copy.95), kind=kOutput, calls=%fused_computation.4 | convolution fusion | flops 3624271872 | bytes 28323840
  361.4 9.6 fusion.6
  371.0 2.8 copy.99
  379.4 70.8 %all-reduce.16.cloned.1.call-done = (f32[6,128,128]{1,2,0:T(8,128)}, f32[6,128,128]{1,2,0:T(8,128)}) async-done(((f32[6,128,128]{1,2,0:T(8,128)}, f32[6,128,128]{1,2,0:T(8,128)}), (f32[6,128,128]{1,2,0:T(8,128)}, f32[6,128,128]{1,2,0:T(8,128)})) %all-reduce.16.cloned.1.call-update) | async-done | bytes 786448 | tf_op jit(solution)/shard_map/psum | solution.py:15
  453.6 139.9 %all-reduce.12.cloned.1.call-done = (f32[128,256]{0,1:T(8,128)}, f32[128,256]{0,1:T(8,128)}) async-done(((f32[128,256]{0,1:T(8,128)}, f32[128,256]{0,1:T(8,128)}), (f32[128,256]{0,1:T(8,128)}, f32[128,256]{0,1:T(8,128)})) %all-reduce.12.cloned.1.call-update) | async-done | bytes 262160 | tf_op jit(solution)/shard_map/psum | solution.py:15
  595.6 11.7 cholesky.130
  607.4 9.8 custom-call.13
  617.6 11.7 cholesky.147
  632.1 4.2 while.6
  636.3 19.7 %custom-call.14 = f32[2,128,128]{1,2,0:T(8,128)S(1)} custom-call(f32[2,128,128]{2,1,0:T(8,128)S(1)} %get-tuple-element.45), custom_call_target="InvertDiagBlocksLowerTriangular" | custom-call | tf_op jit(solution)/shard_map/triangular_solve/custom-call.0 | solution.py:86
  659.7 91.2 %all-gather.3.cloned.1.call-done = f32[6,16,128,256]{3,2,0,1:T(8,128)} async-done(((f32[6,1,128,256]{3,2,0,1:T(8,128)}), f32[6,16,128,256]{3,2,0,1:T(8,128)}) %all-gather.3.cloned.1.call-update) | async-done | bytes 12582928 | tf_op jit(solution)/shard_map/all_gather | solution.py:95
  750.9 10.7 copy.104
  761.6 6.6 convolution_subtract_fusion.1
  768.2 2.2 copy-done
  771.4 71.1 %all-reduce.14.cloned.1.call-done = (f32[6,128,128]{1,2,0:T(8,128)}, f32[6,128,128]{1,2,0:T(8,128)}) async-done(((f32[6,128,128]{1,2,0:T(8,128)}, f32[6,128,128]{1,2,0:T(8,128)}), (f32[6,128,128]{1,2,0:T(8,128)}, f32[6,128,128]{1,2,0:T(8,128)})) %all-reduce.14.cloned.1.call-update) | async-done | bytes 786448 | tf_op jit(solution)/shard_map/psum | solution.py:15
  846.2 139.7 %all-reduce.10.cloned.1.call-done = (f32[128,256]{0,1:T(8,128)}, f32[128,256]{0,1:T(8,128)}) async-done(((f32[128,256]{0,1:T(8,128)}, f32[128,256]{0,1:T(8,128)}), (f32[128,256]{0,1:T(8,128)}, f32[128,256]{0,1:T(8,128)})) %all-reduce.10.cloned.1.call-update) | async-done | bytes 262160 | tf_op jit(solution)/shard_map/psum | solution.py:15
  987.9 11.7 cholesky.164
  999.7 9.8 custom-call.15
  1010.0 11.7 cholesky.181
  1024.5 4.2 while.7
  1028.8 19.7 %custom-call.16 = f32[2,128,128]{1,2,0:T(8,128)S(1)} custom-call(f32[2,128,128]{2,1,0:T(8,128)S(1)} %get-tuple-element.46), custom_call_target="InvertDiagBlocksLowerTriangular" | custom-call | tf_op jit(solution)/shard_map/triangular_solve/custom-call.0 | solution.py:86
  1053.7 89.5 %all-gather.5.cloned.1.call-done = f32[6,16,128,256]{3,2,0,1:T(8,128)} async-done(((f32[6,1,128,256]{3,2,0,1:T(8,128)}), f32[6,16,128,256]{3,2,0,1:T(8,128)}) %all-gather.5.cloned.1.call-update) | async-done | bytes 12582928 | tf_op jit(solution)/shard_map/all_gather | solution.py:95
  1143.2 10.8 copy.110
  1156.2 6.3 convolution_subtract_fusion
  1166.0 12.1 %copy.117 = f32[6,1,128,12,1,128]{5,4,3,2,1,0:T(1,128)} copy(f32[6,1,128,12,1,128]{2,5,0,3,4,1:T(8,128)} %fusion.22) | data formatting | bytes 9437184 | tf_op jit(solution)/shard_map/scatter | solution.py:126
  (116 shorter events, 45.2 us)
Async XLA Ops:
  200.7 8.3 copy-start.4
  200.7 133.4 %all-to-all-start = ((f32[3,16,64,768]{3,2,0,1:T(8,128)}), f32[3,16,64,768]{3,2,0,1:T(8,128)}, u32[]{:S(2)}, u32[]{:S(2)}) async-start(f32[3,16,64,768]{3,2,0,1:T(8,128)} %copy.96), calls=%async_computation | async-start | bytes 18874368 | tf_op jit(solution)/shard_map/all_to_all | solution.py:36
  208.4 241.8 %all-reduce.16.cloned.1.call-start = ((), (), s32[]{:S(2)}) async-start(), calls=%async_computation.6 | async-start | bytes 1572864 | tf_op jit(solution)/shard_map/psum | solution.py:15
  371.0 3.8 copy-start.2
  376.1 2.2 copy-start.1
  379.3 214.3 %all-reduce.12.cloned.1.call-start = ((), (), s32[]{:S(2)}) async-start(), calls=%async_computation.4 | async-start | bytes 524288 | tf_op jit(solution)/shard_map/psum | solution.py:15
  453.0 297.8 %all-gather.3.cloned.1.call-start = ((), (), s32[]{:S(2)}) async-start(), calls=%async_computation.1 | async-start | bytes 13369344 | tf_op jit(solution)/shard_map/all_gather | solution.py:95
  659.3 183.3 %all-reduce.14.cloned.1.call-start = ((), (), s32[]{:S(2)}) async-start(), calls=%async_computation.5 | async-start | bytes 1572864 | tf_op jit(solution)/shard_map/psum | solution.py:15
  768.2 2.2 copy-start
  771.4 214.5 %all-reduce.10.cloned.1.call-start = ((), (), s32[]{:S(2)}) async-start(), calls=%async_computation.3 | async-start | bytes 524288 | tf_op jit(solution)/shard_map/psum | solution.py:15
  845.4 297.8 %all-gather.5.cloned.1.call-start = ((), (), s32[]{:S(2)}) async-start(), calls=%async_computation.2 | async-start | bytes 13369344 | tf_op jit(solution)/shard_map/all_gather | solution.py:95
  1010.0 41.7 %copy-start.3 = (f32[768,256]{1,0:T(8,128)S(1)}, f32[768,256]{1,0:T(8,128)}, u32[]{:S(2)}) copy-start(f32[768,256]{1,0:T(8,128)} %copy.103) | copy-start | bytes 2359300
Sparse Core Ops, SparseCore 0:
  379.4 70.7 all-reduce.15
  453.2 140.3 all-reduce.11
  659.4 91.4 all-gather.2
  771.5 71.0 all-reduce.13
  845.5 140.3 all-reduce.9
  1051.7 91.4 all-gather.4
where the time goes:
time: 1200 us; the launch traced here: 1190 us
  waiting for transfers between devices  715 us (60%)
  other arithmetic  282 us (24%)
  local copies, waits for them, and re-layouts  121 us (10%)
  matrix products  40.6 us (3%)
  between operations  16.8 us (1%)
    psum x4, waiting for transfers between devices, spread_2(): return lax.psum(kept, axis)  422 us
    all_gather x2, waiting for transfers between devices, body(): gathered = lax.all_gather(rows_factor[:, None], 'wide', axis=1, tiled=True)  181 us
    unnamed x1, other arithmetic  167 us
    all_to_all x1, waiting for transfers between devices, body(): lax.all_to_all(pieces, 'wide', split_axis=1, concat_axis=1, tiled=True)  112 us
    another operation x14, other arithmetic, body(): factor = jnp.linalg.cholesky(diagonal)  69.4 us
    another operation x5, other arithmetic, body(): lax.linalg.triangular_solve(factor, panel_cols.reshape(row_blocks * BLOCK...  39.4 us
    reshape x2, local copies, waits for them, and re-layouts, body(): child_update.reshape(pair_blocks, wide_count, HALF, col_blocks * HALF)  27.4 us
  transfers between devices with their start and end apart: 7, of which 7 were waited for; matrix products, arithmetic and copies ran while one was open for 1% of the time, Pallas kernels for 0%

commit v1 on v0

v1 whole, which is shorter than its diff:
```python
import functools

import jax
import jax.numpy as jnp
from jax import lax
from jax.experimental import pallas as pl
from jax.experimental.pallas import tpu as pltpu
from jax.sharding import PartitionSpec as P

BLOCK = 128
HALF = 64
ROW_BLOCKS = 6
COL_BLOCKS = 12
CHILDREN = 8
N_WIDE = 16
N_NARROW = 8
SPAN = 512
CHUNK = HALF * COL_BLOCKS
MESH = pl.DeviceIdType.MESH
F32 = jnp.float32
BF16 = jnp.bfloat16


def mod(value, n):
    return lax.rem(value, n)


def shift_of(p, q):
    return p // 8 + (mod(p, 8) > q).astype(jnp.int32)


def halves(value):
    high = value.astype(BF16)
    low = (value - high.astype(F32)).astype(BF16)
    return high, low


def dot3(a, b, dims):
    ah, al = halves(a)
    bh, bl = halves(b)
    spec = (dims, ((), ()))
    total = lax.dot_general(ah, bh, spec, preferred_element_type=F32)
    total += lax.dot_general(ah, bl, spec, preferred_element_type=F32)
    total += lax.dot_general(al, bh, spec, preferred_element_type=F32)
    return total


def dot_full(a, b, dims):
    return lax.dot_general(
        a, b, (dims, ((), ())), precision=lax.Precision.HIGHEST, preferred_element_type=F32
    )


def thirds(value):
    high = value.astype(BF16).astype(F32)
    rest = value - high
    mid = rest.astype(BF16).astype(F32)
    low = rest - mid
    return high, mid, low


def factor_128(pair):
    lane = lax.broadcasted_iota(jnp.int32, (8, 128), 1)
    sub = lax.broadcasted_iota(jnp.int32, (8, 128), 0)

    def step(b, carry):
        first = pl.multiple_of(b * 8, 8)
        rows = pair[pl.ds(first, 8), :]
        rows_a = rows[:, :128]
        rows_b = rows[:, 128:]
        turned = pltpu.roll(rows_a, mod(128 - first, 128), 1)
        cols = [jnp.broadcast_to(turned[:, j : j + 1], (8, 128)) for j in range(8)]
        e = {}
        for a in range(8):
            for j in range(a + 1):
                e[a, j] = jnp.broadcast_to(cols[j][a : a + 1, :], (8, 128))
        inv = []
        low = {}
        for j in range(8):
            d = e[j, j]
            r = lax.rsqrt(d)
            r = r * (1.5 - 0.5 * d * r * r)
            inv.append(r)
            for a in range(j + 1, 8):
                low[a, j] = e[a, j] * r
            for a in range(j + 1, 8):
                for c in range(j + 1, a + 1):
                    e[a, c] = e[a, c] - low[a, j] * low[c, j]
        ups_a = []
        ups_b = []
        out_a = jnp.zeros((8, 128), F32)
        out_b = jnp.zeros((8, 128), F32)
        for a in range(8):
            row_a = jnp.broadcast_to(rows_a[a : a + 1, :], (8, 128))
            row_b = jnp.broadcast_to(rows_b[a : a + 1, :], (8, 128))
            for j in range(a):
                row_a = row_a - low[a, j] * ups_a[j]
                row_b = row_b - low[a, j] * ups_b[j]
            row_a = row_a * inv[a]
            row_b = row_b * inv[a]
            ups_a.append(row_a)
            ups_b.append(row_b)
            out_a = jnp.where(sub == a, row_a, out_a)
            out_b = jnp.where(sub == a, row_b, out_b)
        done = jnp.concatenate([out_a, out_b], axis=1)
        pair[pl.ds(first, 8), :] = done
        mult = jnp.where(lane >= first + 8, out_a, 0.0)
        mh, mm, ml = thirds(mult)
        uh, um, ul = thirds(done)
        left = jnp.concatenate([mh, mh, mm, mh, ml, mm], axis=0).astype(BF16)
        right = jnp.concatenate([uh, um, uh, ul, uh, um], axis=0).astype(BF16)
        gone = lax.dot_general(
            left, right, (((0,), (0,)), ((), ())), preferred_element_type=F32
        )
        pair[...] = pair[...] - gone
        return carry

    lax.fori_loop(0, 16, step, 0)


def factor_block(jb, work, pair):
    at = jb * 128
    eye = (
        lax.broadcasted_iota(jnp.int32, (128, 128), 0)
        == lax.broadcasted_iota(jnp.int32, (128, 128), 1)
    ).astype(F32)
    pair[:, 0:128] = work[at : at + 128, at : at + 128]
    pair[:, 128:256] = eye
    factor_128(pair)
    inverse = pair[:, 128:256]
    if jb:
        work[at : at + 128, SPAN : SPAN + at] = dot_full(
            inverse, work[at : at + 128, SPAN : SPAN + at], ((1,), (0,))
        )
    work[at : at + 128, SPAN + at : SPAN + at + 128] = inverse
    if jb < 3:
        rest = at + 128
        above = dot_full(inverse, work[at : at + 128, rest:SPAN], ((1,), (0,)))
        work[rest:SPAN, rest:SPAN] -= dot_full(above, above, ((0,), (0,)))
        work[rest:SPAN, SPAN : SPAN + rest] -= dot_full(
            above, work[at : at + 128, SPAN : SPAN + rest], ((0,), (0,))
        )


def kernel(
    child_map, child, root, out,
    marks, row_offs, col_places, chunk_buf, front, bulk_out, bulk_in, unit_in, front_out, front_in, cols, diag, rows, work,
    pair, wide_buf, pick, rows_f, rows_h, rows_l, cols_h, cols_l,
    s_marks, s_chunk, s_front, s_out, bulk_s, bulk_r, unit_s, unit_r, front_s, front_r,
    cols_s, cols_r, hand_s, dz_s, dz_r, dy_s, dy_r, r1_s, r1_r, rz_s, rz_r, ry_s, ry_r,
):
    p = lax.axis_index("wide")
    q = lax.axis_index("narrow")
    core = mod(p, 2)
    chip = p // 2
    ph = p // 8
    pl8 = mod(p, 8)
    zl = q // 4
    y = mod(q, 4)
    own = pl8 == q
    shift = shift_of(p, q)
    q_other = mod(q + 4, 8)

    def remote(src, dst, ssem, rsem, wide, narrow):
        return pltpu.make_async_remote_copy(
            src_ref=src, dst_ref=dst, send_sem=ssem, recv_sem=rsem,
            device_id=(wide, narrow), device_id_type=MESH,
        )

    def local(src, dst, sem):
        return pltpu.make_async_copy(src, dst, sem)

    def chunk_of(n):
        k = n // 16
        late = jnp.where(n < 4, n, 4 + mod(p + n, 12))
        dest = jnp.where(n < 16, late, mod(p + n, 16))
        return k, dest

    def chunk_copy(n):
        k, dest = chunk_of(n)
        at = pl.multiple_of((k * 16 + dest) * CHUNK, CHUNK)
        slot = mod(n, 4)
        to = pl.multiple_of(slot * CHUNK, CHUNK)
        return local(child.at[pl.ds(at, CHUNK)], chunk_buf.at[pl.ds(to, CHUNK)], s_chunk.at[slot])

    for n in range(4):
        chunk_copy(jnp.int32(n)).start()
    marks_load = local(child_map, marks, s_marks.at[0])
    marks_load.start()
    front_load = local(root, front, s_front.at[0])
    front_load.start()

    barrier = pltpu.get_barrier_semaphore()

    def greet(wide, narrow):
        pl.semaphore_signal(barrier, inc=1, device_id=(wide, narrow), device_id_type=MESH)

    def greet_wide(i, carry):
        greet(mod(p + i, 16), q)
        return carry

    lax.fori_loop(1, 16, greet_wide, 0)
    for i in range(1, 4):
        greet(p, zl * 4 + mod(y + i, 4))
    greet(p, q_other)
    pl.semaphore_wait(barrier, 19)

    def packed(n, la, lb):
        base = mod(n, 4) * CHUNK
        xa = chunk_buf[pl.ds(base + la, HALF, stride=COL_BLOCKS), :]
        xb = chunk_buf[pl.ds(base + lb, HALF, stride=COL_BLOCKS), :]
        return jnp.concatenate([xa, xb], axis=1)

    def next_chunk(n):
        @pl.when(n + 4 < 48)
        def _():
            chunk_copy(n + 4).start()

    def unit_copy(u):
        slot = u // 8
        owner = mod(u, 8) * 2 + (slot > 0).astype(jnp.int32)
        return owner, remote(
            bulk_out.at[mod(u, 4) * 3, u // 4], unit_in.at[slot * 8 + chip], unit_s.at[u], unit_r.at[slot * 8 + chip],
            owner, q,
        )

    def front_copy(m):
        u = m * 4 + p
        slot = u // 8
        owner = mod(u, 8) * 2 + (slot > 0).astype(jnp.int32)
        return owner, slot, remote(
            front_out.at[m], front_in.at[slot], front_s.at[m], front_r.at[slot], owner, q
        )

    def bulk_copy(k, dest):
        kk = 2 * k + core
        return remote(
            bulk_out.at[dest * 3 + k], bulk_in.at[kk * 8 + chip],
            bulk_s.at[dest * 3 + k], bulk_r.at[kk * 8 + chip], dest, q,
        )

    def panel_row(kk, dest):
        return jnp.logical_and(kk == 0, dest < 4)

    def pack(n, carry):
        chunk_copy(n).wait()
        k, dest = chunk_of(n)

        def one(m, c):
            bulk_out[dest * 3 + k, m] = packed(n, 2 * m, 2 * m + 1)
            return c

        lax.fori_loop(0, 6, one, 0)

        @pl.when(panel_row(2 * k + core, dest))
        def _():
            def unit(m, c):
                u = m * 4 + dest
                owner, copy = unit_copy(u)

                @pl.when(owner != p)
                def _():
                    copy.start()

                @pl.when(owner == p)
                def _():
                    unit_in[(u // 8) * 8 + chip] = bulk_out[dest * 3, m]
                return c

            lax.fori_loop(0, 6, unit, 0)
        next_chunk(n)
        return carry

    def fire(n, carry):
        k, dest = chunk_of(n)
        kk = 2 * k + core

        @pl.when(jnp.logical_not(panel_row(kk, dest)))
        def _():
            @pl.when(dest != p)
            def _():
                bulk_copy(k, dest).start()

            @pl.when(dest == p)
            def _():
                bulk_in[kk * 8 + chip] = bulk_out[dest * 3 + k]
        return carry

    lax.fori_loop(0, 4, pack, 0)
    front_load.wait()

    @pl.when(p < 4)
    def _():
        def one(m, c):
            for h in range(2):
                front_out[m, :, h * 128 : h * 128 + 128] = front[
                    pl.ds(2 * m + h, BLOCK, stride=COL_BLOCKS), :
                ]
            owner, slot, copy = front_copy(m)

            @pl.when(owner != p)
            def _():
                copy.start()

            @pl.when(owner == p)
            def _():
                front_in[slot] = front_out[m]
            return c

        lax.fori_loop(0, 6, one, 0)

    level = lax.broadcasted_iota(jnp.int32, (128, 128), 0)

    def set_pick(row):
        for j in range(4):
            table = jnp.where(row_offs[row, j : j + 1, :] == level, 1.0, 0.0).astype(BF16)
            pick[:, j * 128 : j * 128 + 128] = table
            pick[:, 512 + j * 128 : 640 + j * 128] = table

    def assemble(source, m):
        for g in range(CHILDREN):
            value = source(g)
            for h in range(2):
                place = jnp.broadcast_to(col_places[2 * m + h, g : g + 1, :], (HALF, 128))
                taken = jnp.take_along_axis(
                    value, jnp.maximum(place, 0), axis=1, mode="promise_in_bounds"
                )
                high, low = halves(jnp.where(place >= 0, taken, 0.0))
                wide_buf[g * 64 : g * 64 + 64, h * 128 : h * 128 + 128] = high
                wide_buf[512 + g * 64 : 576 + g * 64, h * 128 : h * 128 + 128] = low
        return jnp.dot(pick[...], wide_buf[...], preferred_element_type=F32)

    def cols_at(u):
        return cols.at[u // 4, pl.ds(pl.multiple_of(mod(u, 4) * 128, 128), 128), :]

    def cols_copy(u, dc):
        return remote(
            cols_at(u), cols_at(u), cols_s.at[(u // 8) * 8 + dc], cols_r.at[u],
            mod(chip + dc, 8) * 2 + core, q,
        )

    def hand_copy(u):
        return remote(cols_at(u), cols_at(u), hand_s.at[u], cols_r.at[u], chip * 2 + 1 - core, q)

    def own_unit(slot, carry):
        u = slot * 8 + chip
        block = mod(u, 4)

        def landed(g, c):
            @pl.when(jnp.logical_or(core == 1, g != chip))
            def _():
                remote(
                    bulk_out.at[0, 0], unit_in.at[slot * 8 + g], unit_s.at[0],
                    unit_r.at[slot * 8 + g], g * 2, q,
                ).wait_recv()
            return c

        lax.fori_loop(0, 8, landed, 0)

        @pl.when(block != p)
        def _():
            remote(
                front_out.at[0], front_in.at[slot], front_s.at[0], front_r.at[slot], block, q
            ).wait_recv()

        set_pick(6)
        total = assemble(lambda g: unit_in[slot * 8 + g], u // 4)
        cols[u // 4, pl.ds(pl.multiple_of(block * 128, 128), 128), :] = total + front_in[slot]

        def send(dc, c):
            cols_copy(u, dc).start()
            return c

        lax.fori_loop(1, 8, send, 0)
        hand_copy(u).start()
        return carry

    def hand_on(u, carry):
        @pl.when(mod(u, 8) != chip)
        def _():
            cols_copy(u, 1).wait_recv()
            hand_copy(u).start()
        return carry

    def taken(u, carry):
        hand_copy(u).wait_recv()
        return carry

    first_slot = core
    last_slot = 1 + 2 * core

    marks_load.wait()
    lanes = lax.broadcasted_iota(jnp.int32, (CHILDREN, 128), 1)

    def block_marks(block):
        at = pl.multiple_of((block // 2) * 128, 128)
        part = marks[:, pl.ds(at, 128)]
        turned = pltpu.roll(part, 64, 1)
        return (
            jnp.where(mod(block, 2) == 0, part, turned) - block * BLOCK,
            jnp.where(mod(block, 2) == 0, turned, part) - block * BLOCK,
        )

    def row_table(i, carry):
        block = jnp.where(i < 6, i * 16 + p, mod(chip, 4))
        first, second = block_marks(block)
        for j in range(4):
            row_offs[i, j : j + 1, :] = jnp.where(
                lanes[0:1] < 64, first[2 * j : 2 * j + 1], second[2 * j + 1 : 2 * j + 2]
            )
        return carry

    lax.fori_loop(0, 7, row_table, 0)
    ranks = lax.broadcasted_iota(jnp.int32, (HALF, 128), 0)
    spots = lax.broadcasted_iota(jnp.int32, (HALF, 128), 1)

    def col_table(l, carry):
        first, _ = block_marks(l * 8 + q)
        tall = first.T
        for g in range(CHILDREN):
            hit = jnp.broadcast_to(tall[0:HALF, g : g + 1], (HALF, 128)) == spots
            place = jnp.where(hit, ranks + mod(l, 2) * HALF, -1)
            col_places[l, g : g + 1, :] = jnp.max(place, axis=0, keepdims=True)
        return carry

    lax.fori_loop(0, 12, col_table, 0)
    lax.fori_loop(4, 16, pack, 0)
    lax.fori_loop(0, 8, fire, 0)
    lax.fori_loop(first_slot, last_slot, own_unit, 0)
    lax.fori_loop(8, 12, fire, 0)
    lax.fori_loop(16, 24, pack, 0)

    @pl.when(core == 0)
    def _():
        lax.fori_loop(0, 4, hand_on, 0)

    @pl.when(core == 1)
    def _():
        lax.fori_loop(0, 4, taken, 0)

    dz = remote(diag.at[y], diag.at[y], dz_s.at[0], dz_r.at[0], p, q_other)

    @pl.when(zl == 0)
    def _():
        diag[y] = cols[0, :, 0:128]
        dz.start()

    @pl.when(zl == 1)
    def _():
        dz.wait_recv()

    def dy(i):
        return remote(diag.at[y], diag.at[y], dy_s.at[i], dy_r.at[y], p, zl * 4 + mod(y + i, 4))

    for i in range(1, 4):
        dy(i).start()

    lax.fori_loop(12, 16, fire, 0)
    lax.fori_loop(24, 48, pack, 0)

    @pl.when(core == 0)
    def _():
        lax.fori_loop(4, 8, hand_on, 0)
        lax.fori_loop(8, 24, taken, 0)

    @pl.when(core == 1)
    def _():
        lax.fori_loop(8, 24, hand_on, 0)
        lax.fori_loop(4, 8, taken, 0)

    def r1(c):
        return remote(
            cols.at[:, pl.ds(c * 128, 128), pl.ds(pl.multiple_of(ph * 128, 128), 128)],
            rows.at[c], r1_s.at[c], r1_r.at[0], p, zl * 4 + c,
        )

    rz = remote(rows.at[y], rows.at[y], rz_s.at[0], rz_r.at[0], p, q_other)

    def ry(i):
        return remote(rows.at[y], rows.at[y], ry_s.at[i], ry_r.at[y], p, zl * 4 + mod(y + i, 4))

    @pl.when(own)
    def _():
        for c in range(4):
            @pl.when(y != c)
            def _():
                r1(c).start()

            @pl.when(y == c)
            def _():
                rows[c] = cols[:, c * 128 : c * 128 + 128, pl.ds(pl.multiple_of(ph * 128, 128), 128)]

    lax.fori_loop(16, 20, fire, 0)

    for i in range(1, 4):
        src = mod(y + i, 4)
        remote(diag.at[src], diag.at[src], dy_s.at[i], dy_r.at[src], p, q_other).wait_recv()

    for c in range(4):
        work[:, c * 128 : c * 128 + 128] = diag[c]
    full = work[:, 0:SPAN]
    work[:, 0:SPAN] = 0.5 * (full + full.T)
    work[:, SPAN:] = jnp.zeros((SPAN, SPAN), F32)

    factor_block(0, work, pair)

    holder = zl == pl8 // 4

    @pl.when(holder)
    def _():
        @pl.when(jnp.logical_not(own))
        def _():
            remote(
                rows.at[y], rows.at[y], r1_s.at[0], r1_r.at[0], p, q_other
            ).wait_recv()
        rz.start()

    lax.fori_loop(20, 26, fire, 0)
    factor_block(1, work, pair)

    @pl.when(jnp.logical_not(holder))
    def _():
        rz.wait_recv()

    for i in range(1, 4):
        ry(i).start()

    lax.fori_loop(26, 48, fire, 0)
    factor_block(2, work, pair)
    factor_block(3, work, pair)

    def sent_unit(slot, carry):
        u = slot * 8 + chip

        def one(dc, c):
            cols_copy(u, dc).wait_send()
            return c

        lax.fori_loop(1, 8, one, 0)
        hand_copy(u).wait_send()
        return carry

    lax.fori_loop(first_slot, last_slot, sent_unit, 0)

    def handed(u, carry):
        @pl.when(mod(u, 8) != chip)
        def _():
            hand_copy(u).wait_send()
        return carry

    @pl.when(core == 0)
    def _():
        lax.fori_loop(0, 8, handed, 0)

    @pl.when(core == 1)
    def _():
        lax.fori_loop(8, 24, handed, 0)

    @pl.when(zl == 0)
    def _():
        dz.wait_send()

    for i in range(1, 4):
        dy(i).wait_send()

    @pl.when(own)
    def _():
        for c in range(4):
            @pl.when(y != c)
            def _():
                r1(c).wait_send()

    @pl.when(holder)
    def _():
        rz.wait_send()

    for i in range(1, 4):
        ry(i).wait_send()

    for i in range(1, 4):
        src = mod(y + i, 4)
        remote(rows.at[src], rows.at[src], ry_s.at[i], ry_r.at[src], p, q_other).wait_recv()

    def solve_rows(kk, carry):
        block = jnp.concatenate([rows[c, kk] for c in range(4)], axis=0)
        turned = dot3(work[:, SPAN:], block, ((1,), (0,))).T
        at = pl.multiple_of(kk * 128, 128)
        high, low = halves(turned)
        rows_h[pl.ds(at, 128), :] = high
        rows_l[pl.ds(at, 128), :] = low
        for c in range(4):
            rows_f[c, pl.ds(at, 128), :] = turned[:, c * 128 : c * 128 + 128]
        return carry

    lax.fori_loop(0, 6, solve_rows, 0)

    def solve_cols(m, carry):
        solved = dot3(work[:, SPAN:], cols[m], ((1,), (0,)))
        high, low = halves(solved)
        cols[m] = solved
        cols_h[m] = high
        cols_l[m] = low
        return carry

    lax.fori_loop(0, 6, solve_cols, 0)

    def store(kk):
        at = pl.multiple_of(kk * (128 * COL_BLOCKS), 128 * COL_BLOCKS)
        span = pl.ds(at, 128 * COL_BLOCKS)
        return local(front.at[span], out.at[span], s_out.at[kk])

    def finish(kk, carry):
        at = pl.multiple_of(kk * 128, 128)
        panel = panel_row(kk, p)

        @pl.when(jnp.logical_not(panel))
        def _():
            def landed(g, c):
                @pl.when(jnp.logical_not(jnp.logical_and(g == chip, mod(kk, 2) == core)))
                def _():
                    remote(
                        bulk_out.at[0], bulk_in.at[kk * 8 + g], bulk_s.at[0],
                        bulk_r.at[kk * 8 + g], g * 2 + mod(kk, 2), q,
                    ).wait_recv()
                return c

            lax.fori_loop(0, 8, landed, 0)
            set_pick(kk)

            def one(m, c):
                total = assemble(lambda g: bulk_in[kk * 8 + g, m], m)
                high = rows_h[pl.ds(at, 128), :]
                total -= jnp.dot(high, cols_h[m], preferred_element_type=F32)
                total -= jnp.dot(high, cols_l[m], preferred_element_type=F32)
                total -= jnp.dot(rows_l[pl.ds(at, 128), :], cols_h[m], preferred_element_type=F32)
                for h in range(2):
                    where = pl.ds(kk * (128 * COL_BLOCKS) + 2 * m + h, BLOCK, stride=COL_BLOCKS)
                    front[where, :] = front[where, :] + total[:, h * 128 : h * 128 + 128]
                return c

            lax.fori_loop(0, 6, one, 0)

        @pl.when(panel)
        def _():
            for l in range(COL_BLOCKS):
                @pl.when(l * 8 + q > p)
                def _():
                    front[pl.ds(l, BLOCK, stride=COL_BLOCKS), :] = cols[
                        l // 2, pl.ds(pl.multiple_of(p * 128, 128), 128),
                        (l % 2) * 128 : (l % 2) * 128 + 128,
                    ]

        @pl.when(jnp.logical_and(q < 4, kk * 16 + p > q))
        def _():
            front[pl.ds(kk * (128 * COL_BLOCKS), BLOCK, stride=COL_BLOCKS), :] = rows_f[
                q, pl.ds(at, 128), :
            ]

        @pl.when(jnp.logical_and(q < 4, kk * 16 + p == q))
        def _():
            tile = rows_f[q, 0:128, :]
            lower = lax.broadcasted_iota(jnp.int32, (128, 128), 0) >= lax.broadcasted_iota(
                jnp.int32, (128, 128), 1
            )
            front[pl.ds(0, BLOCK, stride=COL_BLOCKS), :] = jnp.where(lower, tile, tile.T)

        store(kk).start()
        return carry

    lax.fori_loop(0, 6, finish, 0)

    def sent_bulk(n, carry):
        k, dest = chunk_of(n)

        @pl.when(jnp.logical_not(jnp.logical_or(dest == p, panel_row(2 * k + core, dest))))
        def _():
            bulk_copy(k, dest).wait_send()
        return carry

    lax.fori_loop(0, 48, sent_bulk, 0)

    @pl.when(core == 0)
    def _():
        def one(u, c):
            owner, copy = unit_copy(u)

            @pl.when(owner != p)
            def _():
                copy.wait_send()
            return c

        lax.fori_loop(0, 24, one, 0)

    @pl.when(p < 4)
    def _():
        def one(m, c):
            owner, slot, copy = front_copy(m)

            @pl.when(owner != p)
            def _():
                copy.wait_send()
            return c

        lax.fori_loop(0, 6, one, 0)

    def stored(kk, carry):
        store(kk).wait()
        return carry

    lax.fori_loop(0, 6, stored, 0)


def plain_copy(src, dst):
    dst[...] = src[...]


def body(root_front, child_update, child_map):
    child = child_update.reshape(3 * 16 * CHUNK, HALF)
    root = root_front.reshape(ROW_BLOCKS * BLOCK * COL_BLOCKS, BLOCK)
    vmem = lambda *shape: pltpu.VMEM(shape, F32)
    sems = lambda n: pltpu.SemaphoreType.DMA((n,))
    out = pl.pallas_call(
        kernel,
        out_shape=jax.ShapeDtypeStruct(root.shape, F32),
        in_specs=[pl.BlockSpec(memory_space=pl.ANY)] * 3,
        out_specs=pl.BlockSpec(memory_space=pl.ANY),
        scratch_shapes=[
            pltpu.VMEM((CHILDREN, 6144), jnp.int32),
            pltpu.VMEM((8, 4, 128), jnp.int32),
            pltpu.VMEM((COL_BLOCKS, CHILDREN, 128), jnp.int32),
            vmem(4 * CHUNK, HALF),
            vmem(ROW_BLOCKS * BLOCK * COL_BLOCKS, BLOCK),
            vmem(48, 6, HALF, 128),
            vmem(48, 6, HALF, 128),
            vmem(24, HALF, 128),
            vmem(6, BLOCK, 256),
            vmem(3, BLOCK, 256),
            vmem(6, SPAN, 256),
            vmem(4, SPAN, 128),
            vmem(4, 6, BLOCK, BLOCK),
            vmem(SPAN, 2 * SPAN),
            vmem(BLOCK, 2 * BLOCK),
            pltpu.VMEM((1024, 256), BF16),
            pltpu.VMEM((BLOCK, 1024), BF16),
            vmem(4, 768, BLOCK),
            pltpu.VMEM((768, SPAN), BF16),
            pltpu.VMEM((768, SPAN), BF16),
            pltpu.VMEM((6, SPAN, 256), BF16),
            pltpu.VMEM((6, SPAN, 256), BF16),
            sems(1), sems(4), sems(1), sems(6), sems(48), sems(48), sems(24), sems(24),
            sems(6), sems(3), sems(24), sems(24), sems(24), sems(1), sems(1), sems(4), sems(4),
            sems(4), sems(1), sems(1), sems(1), sems(4), sems(4),
        ],
        compiler_params=pltpu.CompilerParams(
            collective_id=0, has_side_effects=True, vmem_limit_bytes=60 * 2**20
        ),
    )(child_map, child, root)
    part = pl.BlockSpec((BLOCK * COL_BLOCKS, BLOCK), lambda i: (i, 0))
    out = pl.pallas_call(
        plain_copy,
        grid=(ROW_BLOCKS,),
        out_shape=jax.ShapeDtypeStruct(root.shape, F32),
        in_specs=[part],
        out_specs=part,
    )(out)
    return out.reshape(root_front.shape)


def solution(mesh):
    return jax.shard_map(
        body,
        mesh=mesh,
        in_specs=(
            P(None, "wide", None, None, "narrow", None),
            P("wide", None, None, None, None, "narrow", None),
            P(),
        ),
        out_specs=P(None, "wide", None, None, "narrow", None),
        check_vma=False,
    )
```

time: 1200 us -> 225 us (0.19)
  the two profiles are of different devices: /device:TPU:85 before, /device:TPU:97 now
where the time goes in v1:
time: 225 us
  Pallas kernels  225 us (100%)
    pallas_call x1, Pallas kernels, body(): pl.pallas_call(kernel, out_shape=jax.ShapeDtypeStruct(root.shape, F32), i...  219 us
    pallas_call x1, Pallas kernels, body(): pl.pallas_call(plain_copy, grid=(ROW_BLOCKS,), out_shape=jax.ShapeDtypeSt...  6 us

profile of v1, /device:TPU:97, one launch (start us, length us, event | category | flops | bytes accessed | tf_op | source)
XLA Modules:
  0.0 224.6 jit_solution(16838811781366881521)
XLA Ops:
  0.0 218.5 %shard_map.37.src = f32[9216,128]{1,0:T(8,128)} custom-call(s32[8,6144]{1,0:T(8,128)} %child_map.1, f32[36864,64]{1,0:T(8,128)} %bitcast.3, f32[9216,128]{1,0:T(8,128)} %bitcast.4), custom_call_target="tpu_custom_call" | custom-call | tf_op jit(solution)/shard_map/pallas_call | solution.py:722
  218.6 6.0 %shard_map.38 = f32[9216,128]{1,0:T(8,128)} custom-call(f32[9216,128]{1,0:T(8,128)} %shard_map.37.src), custom_call_target="tpu_custom_call" | custom-call | tf_op jit(solution)/shard_map/pallas_call | solution.py:759

commit v2 on v1

--- a/solution.py
+++ b/solution.py
@@ -33,16 +33,6 @@
     high = value.astype(BF16)
     low = (value - high.astype(F32)).astype(BF16)
     return high, low
-
-
-def dot3(a, b, dims):
-    ah, al = halves(a)
-    bh, bl = halves(b)
-    spec = (dims, ((), ()))
-    total = lax.dot_general(ah, bh, spec, preferred_element_type=F32)
-    total += lax.dot_general(ah, bl, spec, preferred_element_type=F32)
-    total += lax.dot_general(al, bh, spec, preferred_element_type=F32)
-    return total
 
 
 def dot_full(a, b, dims):
@@ -143,10 +133,10 @@
 
 
 def kernel(
-    child_map, child, root, out,
-    marks, row_offs, col_places, chunk_buf, front, bulk_out, bulk_in, unit_in, front_out, front_in, cols, diag, rows, work,
-    pair, wide_buf, pick, rows_f, rows_h, rows_l, cols_h, cols_l,
-    s_marks, s_chunk, s_front, s_out, bulk_s, bulk_r, unit_s, unit_r, front_s, front_r,
+    child_map, child, root, out, bulk_in, row_out, col_out,
+    marks, row_perms, col_places, chunk_buf, front, bulk_out, unit_in, front_out, front_in, cols, diag, rows, work,
+    pair, rows_f, rows_h, rows_l, prod, inv_h, inv_l, relay,
+    keep_s, tab_s, s_marks, s_chunk, s_front, s_out, relay_s, relay_r, bulk_s, bulk_r, unit_s, unit_r, front_s, front_r,
     cols_s, cols_r, hand_s, dz_s, dz_r, dy_s, dy_r, r1_s, r1_r, rz_s, rz_r, ry_s, ry_r,
 ):
     p = lax.axis_index("wide")
@@ -202,8 +192,13 @@
     lax.fori_loop(1, 16, greet_wide, 0)
     for i in range(1, 4):
         greet(p, zl * 4 + mod(y + i, 4))
-    greet(p, q_other)
-    pl.semaphore_wait(barrier, 19)
+
+    def greet_plane(i, carry):
+        greet(i, q_other)
+        return carry
+
+    lax.fori_loop(0, 16, greet_plane, 0)
+    pl.semaphore_wait(barrier, 34)
 
     def packed(n, la, lb):
         base = mod(n, 4) * CHUNK
@@ -232,6 +227,9 @@
             front_out.at[m], front_in.at[slot], front_s.at[m], front_r.at[slot], owner, q
         )
 
+    zh = ph
+    xs = mod(chip, 4)
+
     def bulk_copy(k, dest):
         kk = 2 * k + core
         return remote(
@@ -239,6 +237,46 @@
             bulk_s.at[dest * 3 + k], bulk_r.at[kk * 8 + chip], dest, q,
         )
 
+    def keep_copy(k):
+        return local(bulk_out.at[p * 3 + k], bulk_in.at[(2 * k + core) * 8 + chip], keep_s.at[k])
+
+    def first_copy(k, dest):
+        xd = mod(dest // 2, 4)
+        far = mod(xd - xs + 6, 4) == 0
+        xi = jnp.where(far, mod(xd + 1, 4), xd)
+        gap = mod(xs - xi + 4, 4)
+        way = jnp.where(far, 3, jnp.where(gap == 3, 2, gap))
+        zi = jnp.where(mod(core + xs + k, 2) == 0, zh, 1 - zh)
+        slot = k * 8 + way * 2 + core
+        return remote(
+            bulk_out.at[dest * 3 + k], relay.at[slot], bulk_s.at[dest * 3 + k],
+            relay_r.at[slot], (zi * 4 + xi) * 2 + mod(dest, 2), q_other,
+        )
+
+    def second_copy(k, way, cs):
+        slot = k * 8 + way * 2 + cs
+        side = jnp.where(jnp.logical_or(way == 1, way == 3), 1, jnp.where(way == 2, 3, 0))
+        source_x = mod(xs + side, 4)
+        dest_x = jnp.where(way == 3, mod(xs + 3, 4), xs)
+        source_z = jnp.where(mod(cs + source_x + k, 2) == 0, zh, 1 - zh)
+        dest = ((1 - source_z) * 4 + dest_x) * 2 + core
+        place = (2 * k + cs) * 8 + source_z * 4 + source_x
+        return dest, remote(
+            relay.at[slot], bulk_in.at[place], relay_s.at[slot], bulk_r.at[place], dest, q_other
+        )
+
+    def relay_one(i, carry):
+        k, way, cs = i // 8, mod(i, 8) // 2, mod(i, 2)
+        dest, copy = second_copy(k, way, cs)
+
+        @pl.when(jnp.logical_not(panel_row(2 * k + cs, dest)))
+        def _():
+            remote(
+                bulk_out.at[0], relay.at[i], bulk_s.at[0], relay_r.at[i], p, q_other
+            ).wait_recv()
+            copy.start()
+        return carry
+
     def panel_row(kk, dest):
         return jnp.logical_and(kk == 0, dest < 4)
 
@@ -272,18 +310,24 @@
         return carry
 
     def fire(n, carry):
-        k, dest = chunk_of(n)
+        k, j = n // 16, mod(n, 16)
+        crossing = j < 8
+        dest = jnp.where(crossing, 1 - zh, zh) * 8 + mod(p + j, 8)
         kk = 2 * k + core
 
         @pl.when(jnp.logical_not(panel_row(kk, dest)))
         def _():
-            @pl.when(dest != p)
+            @pl.when(crossing)
+            def _():
+                first_copy(k, dest).start()
+
+            @pl.when(jnp.logical_and(jnp.logical_not(crossing), dest != p))
             def _():
                 bulk_copy(k, dest).start()
 
             @pl.when(dest == p)
             def _():
-                bulk_in[kk * 8 + chip] = bulk_out[dest * 3 + k]
+                keep_copy(k).start()
         return carry
 
     lax.fori_loop(0, 4, pack, 0)
@@ -309,26 +353,23 @@
 
         lax.fori_loop(0, 6, one, 0)
 
-    level = lax.broadcasted_iota(jnp.int32, (128, 128), 0)
-
-    def set_pick(row):
-        for j in range(4):
-            table = jnp.where(row_offs[row, j : j + 1, :] == level, 1.0, 0.0).astype(BF16)
-            pick[:, j * 128 : j * 128 + 128] = table
-            pick[:, 512 + j * 128 : 640 + j * 128] = table
-
-    def assemble(source, m):
-        for g in range(CHILDREN):
-            value = source(g)
-            for h in range(2):
-                place = jnp.broadcast_to(col_places[2 * m + h, g : g + 1, :], (HALF, 128))
-                taken = jnp.take_along_axis(
-                    value, jnp.maximum(place, 0), axis=1, mode="promise_in_bounds"
-                )
-                high, low = halves(jnp.where(place >= 0, taken, 0.0))
-                wide_buf[g * 64 : g * 64 + 64, h * 128 : h * 128 + 128] = high
-                wide_buf[512 + g * 64 : 576 + g * 64, h * 128 : h * 128 + 128] = low
-        return jnp.dot(pick[...], wide_buf[...], preferred_element_type=F32)
+    def assemble(source, m, row):
+        sides = []
+        for h in range(2):
+            total = jnp.zeros((BLOCK, BLOCK), F32)
+            for pair_id in range(CHILDREN // 2):
+                parts = []
+                for g in (2 * pair_id, 2 * pair_id + 1):
+                    place = jnp.broadcast_to(col_places[2 * m + h, g : g + 1, :], (HALF, 128))
+                    taken = jnp.take_along_axis(
+                        source(g), jnp.maximum(place, 0), axis=1, mode="promise_in_bounds"
+                    )
+                    parts.append(jnp.where(place >= 0, taken, 0.0))
+                turned = jnp.concatenate(parts, axis=0).T
+                order = jnp.broadcast_to(row_perms[row, pair_id : pair_id + 1, :], (BLOCK, BLOCK))
+                total += jnp.take_along_axis(turned, order, axis=1, mode="promise_in_bounds")
+            sides.append(total.T)
+        return sides
 
     def cols_at(u):
         return cols.at[u // 4, pl.ds(pl.multiple_of(mod(u, 4) * 128, 128), 128), :]
@@ -363,9 +404,10 @@
                 front_out.at[0], front_in.at[slot], front_s.at[0], front_r.at[slot], block, q
             ).wait_recv()
 
-        set_pick(6)
-        total = assemble(lambda g: unit_in[slot * 8 + g], u // 4)
-        cols[u // 4, pl.ds(pl.multiple_of(block * 128, 128), 128), :] = total + front_in[slot]
+        sides = assemble(lambda g: unit_in[slot * 8 + g], u // 4, 6)
+        cols[u // 4, pl.ds(pl.multiple_of(block * 128, 128), 128), :] = (
+            jnp.concatenate(sides, axis=1) + front_in[slot]
+        )
 
         def send(dc, c):
             cols_copy(u, dc).start()
@@ -390,45 +432,40 @@
     last_slot = 1 + 2 * core
 
     marks_load.wait()
-    lanes = lax.broadcasted_iota(jnp.int32, (CHILDREN, 128), 1)
-
-    def block_marks(block):
+    ranks = lax.broadcasted_iota(jnp.int32, (HALF, 128), 0)
+    spots = lax.broadcasted_iota(jnp.int32, (HALF, 128), 1)
+
+    def places(block):
         at = pl.multiple_of((block // 2) * 128, 128)
         part = marks[:, pl.ds(at, 128)]
-        turned = pltpu.roll(part, 64, 1)
-        return (
-            jnp.where(mod(block, 2) == 0, part, turned) - block * BLOCK,
-            jnp.where(mod(block, 2) == 0, turned, part) - block * BLOCK,
-        )
-
-    def row_table(i, carry):
-        block = jnp.where(i < 6, i * 16 + p, mod(chip, 4))
-        first, second = block_marks(block)
-        for j in range(4):
-            row_offs[i, j : j + 1, :] = jnp.where(
-                lanes[0:1] < 64, first[2 * j : 2 * j + 1], second[2 * j + 1 : 2 * j + 2]
-            )
-        return carry
-
-    lax.fori_loop(0, 7, row_table, 0)
-    ranks = lax.broadcasted_iota(jnp.int32, (HALF, 128), 0)
-    spots = lax.broadcasted_iota(jnp.int32, (HALF, 128), 1)
-
-    def col_table(l, carry):
-        first, _ = block_marks(l * 8 + q)
-        tall = first.T
+        mine = jnp.where(mod(block, 2) == 0, part, pltpu.roll(part, 64, 1)) - block * BLOCK
+        tall = mine.T
+        found = []
         for g in range(CHILDREN):
             hit = jnp.broadcast_to(tall[0:HALF, g : g + 1], (HALF, 128)) == spots
-            place = jnp.where(hit, ranks + mod(l, 2) * HALF, -1)
-            col_places[l, g : g + 1, :] = jnp.max(place, axis=0, keepdims=True)
+            found.append(jnp.max(jnp.where(hit, ranks, -1), axis=0, keepdims=True))
+        return found
+
+    def row_table(i, carry):
+        found = places(jnp.where(i < 6, i * 16 + p, mod(chip, 4)))
+        for j in range(4):
+            first, second = found[2 * j], found[2 * j + 1]
+            row_perms[i, j : j + 1, :] = jnp.where(first >= 0, first, second + HALF)
+        return carry
+
+    lax.fori_loop(0, 7, row_table, 0)
+
+    def col_table(l, carry):
+        found = places(l * 8 + q)
+        for g in range(CHILDREN):
+            col_places[l, g : g + 1, :] = jnp.where(
+                found[g] >= 0, found[g] + mod(l, 2) * HALF, -1
+            )
         return carry
 
     lax.fori_loop(0, 12, col_table, 0)
+    lax.fori_loop(first_slot, last_slot, own_unit, 0)
     lax.fori_loop(4, 16, pack, 0)
-    lax.fori_loop(0, 8, fire, 0)
-    lax.fori_loop(first_slot, last_slot, own_unit, 0)
-    lax.fori_loop(8, 12, fire, 0)
-    lax.fori_loop(16, 24, pack, 0)
 
     @pl.when(core == 0)
     def _():
@@ -455,8 +492,8 @@
     for i in range(1, 4):
         dy(i).start()
 
-    lax.fori_loop(12, 16, fire, 0)
-    lax.fori_loop(24, 48, pack, 0)
+    lax.fori_loop(0, 16, fire, 0)
+    lax.fori_loop(16, 48, pack, 0)
 
     @pl.when(core == 0)
     def _():
@@ -490,7 +527,6 @@
             def _():
                 rows[c] = cols[:, c * 128 : c * 128 + 128, pl.ds(pl.multiple_of(ph * 128, 128), 128)]
 
-    lax.fori_loop(16, 20, fire, 0)
 
     for i in range(1, 4):
         src = mod(y + i, 4)
@@ -515,7 +551,9 @@
             ).wait_recv()
         rz.start()
 
-    lax.fori_loop(20, 26, fire, 0)
+    lax.fori_loop(16, 24, fire, 0)
+    lax.fori_loop(0, 8, relay_one, 0)
+    lax.fori_loop(24, 32, fire, 0)
     factor_block(1, work, pair)
 
     @pl.when(jnp.logical_not(holder))
@@ -525,9 +563,12 @@
     for i in range(1, 4):
         ry(i).start()
 
-    lax.fori_loop(26, 48, fire, 0)
+    lax.fori_loop(32, 40, fire, 0)
     factor_block(2, work, pair)
+    lax.fori_loop(8, 16, relay_one, 0)
+    lax.fori_loop(40, 48, fire, 0)
     factor_block(3, work, pair)
+    lax.fori_loop(16, 24, relay_one, 0)
 
     def sent_unit(slot, carry):
         u = slot * 8 + chip
@@ -581,9 +622,20 @@
         src = mod(y + i, 4)
         remote(rows.at[src], rows.at[src], ry_s.at[i], ry_r.at[src], p, q_other).wait_recv()
 
+    inverse_h, inverse_l = halves(work[:, SPAN:])
+    inv_h[...] = inverse_h
+    inv_l[...] = inverse_l
+
+    def solve(block):
+        high, low = halves(block)
+        total = jnp.dot(inv_h[...], high, preferred_element_type=F32)
+        total += jnp.dot(inv_h[...], low, preferred_element_type=F32)
+        total += jnp.dot(inv_l[...], high, preferred_element_type=F32)
+        return total
+
     def solve_rows(kk, carry):
         block = jnp.concatenate([rows[c, kk] for c in range(4)], axis=0)
-        turned = dot3(work[:, SPAN:], block, ((1,), (0,))).T
+        turned = solve(block).T
         at = pl.multiple_of(kk * 128, 128)
         high, low = halves(turned)
         rows_h[pl.ds(at, 128), :] = high
@@ -595,11 +647,24 @@
     lax.fori_loop(0, 6, solve_rows, 0)
 
     def solve_cols(m, carry):
-        solved = dot3(work[:, SPAN:], cols[m], ((1,), (0,)))
+        solved = solve(cols[m])
         high, low = halves(solved)
         cols[m] = solved
-        cols_h[m] = high
-        cols_l[m] = low
+        total = jnp.dot(rows_h[...], high, preferred_element_type=F32)
+        total += jnp.dot(rows_h[...], low, preferred_element_type=F32)
+        total += jnp.dot(rows_l[...], high, preferred_element_type=F32)
+        prod[...] = total
+
+        def less(kk, c):
+            at = pl.multiple_of(kk * 128, 128)
+            for h in range(2):
+                where = pl.ds(kk * (128 * COL_BLOCKS) + 2 * m + h, BLOCK, stride=COL_BLOCKS)
+                front[where, :] = (
+                    front[where, :] - prod[pl.ds(at, 128), h * 128 : h * 128 + 128]
+                )
+            return c
+
+        lax.fori_loop(0, 6, less, 0)
         return carry
 
     lax.fori_loop(0, 6, solve_cols, 0)
@@ -609,54 +674,26 @@
         span = pl.ds(at, 128 * COL_BLOCKS)
         return local(front.at[span], out.at[span], s_out.at[kk])
 
-    def finish(kk, carry):
-        at = pl.multiple_of(kk * 128, 128)
-        panel = panel_row(kk, p)
-
-        @pl.when(jnp.logical_not(panel))
-        def _():
-            def landed(g, c):
-                @pl.when(jnp.logical_not(jnp.logical_and(g == chip, mod(kk, 2) == core)))
-                def _():
-                    remote(
-                        bulk_out.at[0], bulk_in.at[kk * 8 + g], bulk_s.at[0],
-                        bulk_r.at[kk * 8 + g], g * 2 + mod(kk, 2), q,
-                    ).wait_recv()
-                return c
-
-            lax.fori_loop(0, 8, landed, 0)
-            set_pick(kk)
-
-            def one(m, c):
-                total = assemble(lambda g: bulk_in[kk * 8 + g, m], m)
-                high = rows_h[pl.ds(at, 128), :]
-                total -= jnp.dot(high, cols_h[m], preferred_element_type=F32)
-                total -= jnp.dot(high, cols_l[m], preferred_element_type=F32)
-                total -= jnp.dot(rows_l[pl.ds(at, 128), :], cols_h[m], preferred_element_type=F32)
-                for h in range(2):
-                    where = pl.ds(kk * (128 * COL_BLOCKS) + 2 * m + h, BLOCK, stride=COL_BLOCKS)
-                    front[where, :] = front[where, :] + total[:, h * 128 : h * 128 + 128]
-                return c
-
-            lax.fori_loop(0, 6, one, 0)
-
-        @pl.when(panel)
-        def _():
-            for l in range(COL_BLOCKS):
-                @pl.when(l * 8 + q > p)
-                def _():
-                    front[pl.ds(l, BLOCK, stride=COL_BLOCKS), :] = cols[
-                        l // 2, pl.ds(pl.multiple_of(p * 128, 128), 128),
-                        (l % 2) * 128 : (l % 2) * 128 + 128,
-                    ]
-
-        @pl.when(jnp.logical_and(q < 4, kk * 16 + p > q))
-        def _():
-            front[pl.ds(kk * (128 * COL_BLOCKS), BLOCK, stride=COL_BLOCKS), :] = rows_f[
-                q, pl.ds(at, 128), :
-            ]
-
-        @pl.when(jnp.logical_and(q < 4, kk * 16 + p == q))
+    @pl.when(p < 4)
+    def _():
+        for l in range(COL_BLOCKS):
+            @pl.when(l * 8 + q > p)
+            def _():
+                front[pl.ds(l, BLOCK, stride=COL_BLOCKS), :] = cols[
+                    l // 2, pl.ds(pl.multiple_of(p * 128, 128), 128),
+                    (l % 2) * 128 : (l % 2) * 128 + 128,
+                ]
+
+    @pl.when(q < 4)
+    def _():
+        for kk in range(ROW_BLOCKS):
+            @pl.when(kk * 16 + p > q)
+            def _():
+                front[pl.ds(kk * (128 * COL_BLOCKS), BLOCK, stride=COL_BLOCKS), :] = rows_f[
+                    q, kk * 128 : kk * 128 + 128, :
+                ]
+
+        @pl.when(p == q)
         def _():
             tile = rows_f[q, 0:128, :]
             lower = lax.broadcasted_iota(jnp.int32, (128, 128), 0) >= lax.broadcasted_iota(
@@ -664,10 +701,35 @@
             )
             front[pl.ds(0, BLOCK, stride=COL_BLOCKS), :] = jnp.where(lower, tile, tile.T)
 
-        store(kk).start()
-        return carry
-
-    lax.fori_loop(0, 6, finish, 0)
+    lax.fori_loop(0, 6, lambda kk, c: (store(kk).start(), c)[1], 0)
+
+    def landed(i, carry):
+        kk, g = i // 8, mod(i, 8)
+        mine = jnp.logical_and(g == chip, mod(kk, 2) == core)
+
+        @pl.when(jnp.logical_not(jnp.logical_or(mine, panel_row(kk, p))))
+        def _():
+            remote(
+                bulk_out.at[0], bulk_in.at[i], bulk_s.at[0], bulk_r.at[i], g * 2 + mod(kk, 2), q
+            ).wait_recv()
+        return carry
+
+    lax.fori_loop(0, 48, landed, 0)
+
+    def kept(k, carry):
+        @pl.when(jnp.logical_not(panel_row(2 * k + core, p)))
+        def _():
+            keep_copy(k).wait()
+        return carry
+
+    lax.fori_loop(0, 3, kept, 0)
+    tables = [
+        local(row_perms, row_out, tab_s.at[0]), local(col_places, col_out, tab_s.at[1])
+    ]
+    for copy in tables:
+        copy.start()
+    for copy in tables:
+        copy.wait()
 
     def sent_bulk(n, carry):
         k, dest = chunk_of(n)
@@ -703,6 +765,17 @@
 
         lax.fori_loop(0, 6, one, 0)
 
+    def relayed(i, carry):
+        k, way, cs = i // 8, mod(i, 8) // 2, mod(i, 2)
+        dest, copy = second_copy(k, way, cs)
+
+        @pl.when(jnp.logical_not(panel_row(2 * k + cs, dest)))
+        def _():
+            copy.wait_send()
+        return carry
+
+    lax.fori_loop(0, 24, relayed, 0)
+
     def stored(kk, carry):
         store(kk).wait()
         return carry
@@ -710,8 +783,45 @@
     lax.fori_loop(0, 6, stored, 0)
 
 
-def plain_copy(src, dst):
-    dst[...] = src[...]
+def add_children(row_perms, col_places, front, children, out, pick, wide_buf):
+    kk = pl.program_id(0)
+    p = lax.axis_index("wide")
+    q = lax.axis_index("narrow")
+    panel = jnp.logical_and(kk == 0, p < 4)
+
+    @pl.when(panel)
+    def _():
+        out[...] = front[...]
+
+    @pl.when(jnp.logical_not(panel))
+    def _():
+        level = lax.broadcasted_iota(jnp.int32, (128, 128), 1)
+        for j in range(4):
+            order = jnp.broadcast_to(row_perms[kk, j : j + 1, :], (128, 128)).T
+            table = jnp.where(order == level, 1.0, 0.0).astype(BF16)
+            pick[:, j * 128 : j * 128 + 128] = table
+            pick[:, 512 + j * 128 : 640 + j * 128] = table
+
+        def one(m, carry):
+            for g in range(CHILDREN):
+                for h in range(2):
+                    place = jnp.broadcast_to(col_places[2 * m + h, g : g + 1, :], (HALF, 128))
+                    taken = jnp.take_along_axis(
+                        children[g, m], jnp.maximum(place, 0), axis=1, mode="promise_in_bounds"
+                    )
+                    high, low = halves(jnp.where(place >= 0, taken, 0.0))
+                    wide_buf[g * 64 : g * 64 + 64, h * 128 : h * 128 + 128] = high
+                    wide_buf[512 + g * 64 : 576 + g * 64, h * 128 : h * 128 + 128] = low
+            total = jnp.dot(pick[...], wide_buf[...], preferred_element_type=F32)
+            for h in range(2):
+                where = pl.ds(2 * m + h, BLOCK, stride=COL_BLOCKS)
+                side = total[:, h * 128 : h * 128 + 128]
+                if h == 0:
+                    side = jnp.where(jnp.logical_and(m == 0, q < 4), 0.0, side)
+                out[where, :] = front[where, :] + side
+            return carry
+
+        lax.fori_loop(0, 6, one, 0)
 
 
 def body(root_front, child_update, child_map):
@@ -719,18 +829,22 @@
     root = root_front.reshape(ROW_BLOCKS * BLOCK * COL_BLOCKS, BLOCK)
     vmem = lambda *shape: pltpu.VMEM(shape, F32)
     sems = lambda n: pltpu.SemaphoreType.DMA((n,))
-    out = pl.pallas_call(
+    front, children, row_perms, col_places = pl.pallas_call(
         kernel,
-        out_shape=jax.ShapeDtypeStruct(root.shape, F32),
+        out_shape=[
+            jax.ShapeDtypeStruct(root.shape, F32),
+            jax.ShapeDtypeStruct((48, 6, HALF, 128), F32),
+            jax.ShapeDtypeStruct((8, 4, 128), jnp.int32),
+            jax.ShapeDtypeStruct((COL_BLOCKS, CHILDREN, 128), jnp.int32),
+        ],
         in_specs=[pl.BlockSpec(memory_space=pl.ANY)] * 3,
-        out_specs=pl.BlockSpec(memory_space=pl.ANY),
+        out_specs=[pl.BlockSpec(memory_space=pl.ANY)] * 4,
         scratch_shapes=[
             pltpu.VMEM((CHILDREN, 6144), jnp.int32),
             pltpu.VMEM((8, 4, 128), jnp.int32),
             pltpu.VMEM((COL_BLOCKS, CHILDREN, 128), jnp.int32),
             vmem(4 * CHUNK, HALF),
             vmem(ROW_BLOCKS * BLOCK * COL_BLOCKS, BLOCK),
-            vmem(48, 6, HALF, 128),
             vmem(48, 6, HALF, 128),
             vmem(24, HALF, 128),
             vmem(6, BLOCK, 256),
@@ -740,14 +854,14 @@
             vmem(4, 6, BLOCK, BLOCK),
             vmem(SPAN, 2 * SPAN),
             vmem(BLOCK, 2 * BLOCK),
-            pltpu.VMEM((1024, 256), BF16),
-            pltpu.VMEM((BLOCK, 1024), BF16),
             vmem(4, 768, BLOCK),
             pltpu.VMEM((768, SPAN), BF16),
             pltpu.VMEM((768, SPAN), BF16),
-            pltpu.VMEM((6, SPAN, 256), BF16),
-            pltpu.VMEM((6, SPAN, 256), BF16),
-            sems(1), sems(4), sems(1), sems(6), sems(48), sems(48), sems(24), sems(24),
+            vmem(768, 256),
+            pltpu.VMEM((SPAN, SPAN), BF16),
+            pltpu.VMEM((SPAN, SPAN), BF16),
+            vmem(24, 6, HALF, 128),
+            sems(3), sems(2), sems(1), sems(4), sems(1), sems(6), sems(24), sems(24), sems(48), sems(48), sems(24), sems(24),
             sems(6), sems(3), sems(24), sems(24), sems(24), sems(1), sems(1), sems(4), sems(4),
             sems(4), sems(1), sems(1), sems(1), sems(4), sems(4),
         ],
@@ -757,12 +871,19 @@
     )(child_map, child, root)
     part = pl.BlockSpec((BLOCK * COL_BLOCKS, BLOCK), lambda i: (i, 0))
     out = pl.pallas_call(
-        plain_copy,
+        add_children,
         grid=(ROW_BLOCKS,),
         out_shape=jax.ShapeDtypeStruct(root.shape, F32),
-        in_specs=[part],
+        in_specs=[
+            pl.BlockSpec((8, 4, 128), lambda i: (0, 0, 0)),
+            pl.BlockSpec((COL_BLOCKS, CHILDREN, 128), lambda i: (0, 0, 0)),
+            part,
+            pl.BlockSpec((CHILDREN, 6, HALF, 128), lambda i: (i, 0, 0, 0)),
+        ],
         out_specs=part,
-    )(out)
+        scratch_shapes=[pltpu.VMEM((BLOCK, 1024), BF16), pltpu.VMEM((1024, 256), BF16)],
+        compiler_params=pltpu.CompilerParams(vmem_limit_bytes=40 * 2**20),
+    )(row_perms, col_places, front, children)
     return out.reshape(root_front.shape)
 
 

time: 225 us -> 220 us (0.978)
  the two profiles are of different devices: /device:TPU:97 before, /device:TPU:85 now
where the time goes in v2:
time: 220 us; the launch traced here: 217 us
  Pallas kernels  210 us (95%)
  local copies, waits for them, and re-layouts  7.52 us (3%)
    pallas_call x1, Pallas kernels, body(): pl.pallas_call(kernel, out_shape=[jax.ShapeDtypeStruct(root.shape, F32),...  186 us
    pallas_call x1, Pallas kernels, body(): pl.pallas_call(add_children, grid=(ROW_BLOCKS,), out_shape=jax.ShapeDtype...  24.3 us
    unnamed x8, local copies, waits for them, and re-layouts  7.52 us

profile of v2, /device:TPU:85, one launch (start us, length us, event | category | flops | bytes accessed | tf_op | source)
XLA Modules:
  0.0 217.5 jit_solution(1556240734731410532)
XLA Ops:
  0.0 185.6 %shard_map.37 = (f32[9216,128]{1,0:T(8,128)}, f32[48,6,64,128]{3,2,1,0:T(8,128)}, s32[8,4,128]{2,1,0:T(4,128)}, s32[12,8,128]{2,1,0:T(8,128)}) custom-call(s32[8,6144]{1,0:T(8,128)} %child_map.1, f32[36864,64]{1,0:T(8,128)} %bitcast.3, f32[9216,128]{1,0:T(8,128)} %bitcast.4), custom_call_target="tpu_custom_call" | custom-call | tf_op jit(solution)/shard_map/pallas_call | solution.py:832
  185.6 0.0 copy-start
  185.6 3.7 %copy-done = f32[48,6,64,128]{3,2,1,0:T(8,128)S(1)} copy-done((f32[48,6,64,128]{3,2,1,0:T(8,128)S(1)}, f32[48,6,64,128]{3,2,1,0:T(8,128)}, u32[]{:S(2)}) %copy-start) | copy-done | bytes 9437208
  189.3 0.0 copy-start.1
  189.3 2.3 %copy-done.1 = f32[9216,128]{1,0:T(8,128)S(1)} copy-done((f32[9216,128]{1,0:T(8,128)S(1)}, f32[9216,128]{1,0:T(8,128)}, u32[]{:S(2)}) %copy-start.1) | copy-done | bytes 4718616
  191.6 0.0 copy-start.2
  191.6 0.8 copy-done.2
  192.4 0.0 copy-start.3
  192.4 0.7 copy-done.3
  193.2 24.3 %shard_map.38 = f32[9216,128]{1,0:T(8,128)} custom-call(s32[8,4,128]{2,1,0:T(4,128)S(1)} %copy-done.3, s32[12,8,128]{2,1,0:T(8,128)S(1)} %copy-done.2, f32[9216,128]{1,0:T(8,128)S(1)} %copy-done.1, f32[48,6,64,128]{3,2,1,0:T(8,128)S(1)} %copy-done), custom_call_target="tpu_custom_call" | custom-call | tf_op jit(solution)/shard_map/pallas_call | solution.py:873
Async XLA Ops:
  185.6 3.7 %copy-start = (f32[48,6,64,128]{3,2,1,0:T(8,128)S(1)}, f32[48,6,64,128]{3,2,1,0:T(8,128)}, u32[]{:S(2)}) copy-start(f32[48,6,64,128]{3,2,1,0:T(8,128)} %get-tuple-element.12.children) | copy-start | bytes 28311556
  189.3 2.3 %copy-start.1 = (f32[9216,128]{1,0:T(8,128)S(1)}, f32[9216,128]{1,0:T(8,128)}, u32[]{:S(2)}) copy-start(f32[9216,128]{1,0:T(8,128)} %get-tuple-element.11.front) | copy-start | bytes 14155780
  191.6 0.8 copy-start.2
  192.4 0.7 copy-start.3

commit v3 on v2

--- a/solution.py
+++ b/solution.py
@@ -49,11 +49,13 @@
     return high, mid, low
 
 
-def factor_128(pair):
+def factor_128(pair, beside):
     lane = lax.broadcasted_iota(jnp.int32, (8, 128), 1)
     sub = lax.broadcasted_iota(jnp.int32, (8, 128), 0)
 
     def step(b, carry):
+        beside.begin(b)
+        beside.work(b)
         first = pl.multiple_of(b * 8, 8)
         rows = pair[pl.ds(first, 8), :]
         rows_a = rows[:, :128]
@@ -103,12 +105,13 @@
             left, right, (((0,), (0,)), ((), ())), preferred_element_type=F32
         )
         pair[...] = pair[...] - gone
+        beside.end(b)
         return carry
 
     lax.fori_loop(0, 16, step, 0)
 
 
-def factor_block(jb, work, pair):
+def factor_block(jb, work, pair, beside):
     at = jb * 128
     eye = (
         lax.broadcasted_iota(jnp.int32, (128, 128), 0)
@@ -116,7 +119,7 @@
     ).astype(F32)
     pair[:, 0:128] = work[at : at + 128, at : at + 128]
     pair[:, 128:256] = eye
-    factor_128(pair)
+    factor_128(pair, beside)
     inverse = pair[:, 128:256]
     if jb:
         work[at : at + 128, SPAN : SPAN + at] = dot_full(
@@ -135,8 +138,8 @@
 def kernel(
     child_map, child, root, out, bulk_in, row_out, col_out,
     marks, row_perms, col_places, chunk_buf, front, bulk_out, unit_in, front_out, front_in, cols, diag, rows, work,
-    pair, rows_f, rows_h, rows_l, prod, inv_h, inv_l, relay,
-    keep_s, tab_s, s_marks, s_chunk, s_front, s_out, relay_s, relay_r, bulk_s, bulk_r, unit_s, unit_r, front_s, front_r,
+    pair, rows_f, rows_h, rows_l, prod, inv_h, inv_l,
+    keep_s, tab_s, s_marks, s_chunk, s_front, s_out, bulk_s, bulk_r, unit_s, unit_r, front_s, front_r,
     cols_s, cols_r, hand_s, dz_s, dz_r, dy_s, dy_r, r1_s, r1_r, rz_s, rz_r, ry_s, ry_r,
 ):
     p = lax.axis_index("wide")
@@ -193,12 +196,8 @@
     for i in range(1, 4):
         greet(p, zl * 4 + mod(y + i, 4))
 
-    def greet_plane(i, carry):
-        greet(i, q_other)
-        return carry
-
-    lax.fori_loop(0, 16, greet_plane, 0)
-    pl.semaphore_wait(barrier, 34)
+    greet(p, q_other)
+    pl.semaphore_wait(barrier, 19)
 
     def packed(n, la, lb):
         base = mod(n, 4) * CHUNK
@@ -227,9 +226,6 @@
             front_out.at[m], front_in.at[slot], front_s.at[m], front_r.at[slot], owner, q
         )
 
-    zh = ph
-    xs = mod(chip, 4)
-
     def bulk_copy(k, dest):
         kk = 2 * k + core
         return remote(
@@ -240,43 +236,6 @@
     def keep_copy(k):
         return local(bulk_out.at[p * 3 + k], bulk_in.at[(2 * k + core) * 8 + chip], keep_s.at[k])
 
-    def first_copy(k, dest):
-        xd = mod(dest // 2, 4)
-        far = mod(xd - xs + 6, 4) == 0
-        xi = jnp.where(far, mod(xd + 1, 4), xd)
-        gap = mod(xs - xi + 4, 4)
-        way = jnp.where(far, 3, jnp.where(gap == 3, 2, gap))
-        zi = jnp.where(mod(core + xs + k, 2) == 0, zh, 1 - zh)
-        slot = k * 8 + way * 2 + core
-        return remote(
-            bulk_out.at[dest * 3 + k], relay.at[slot], bulk_s.at[dest * 3 + k],
-            relay_r.at[slot], (zi * 4 + xi) * 2 + mod(dest, 2), q_other,
-        )
-
-    def second_copy(k, way, cs):
-        slot = k * 8 + way * 2 + cs
-        side = jnp.where(jnp.logical_or(way == 1, way == 3), 1, jnp.where(way == 2, 3, 0))
-        source_x = mod(xs + side, 4)
-        dest_x = jnp.where(way == 3, mod(xs + 3, 4), xs)
-        source_z = jnp.where(mod(cs + source_x + k, 2) == 0, zh, 1 - zh)
-        dest = ((1 - source_z) * 4 + dest_x) * 2 + core
-        place = (2 * k + cs) * 8 + source_z * 4 + source_x
-        return dest, remote(
-            relay.at[slot], bulk_in.at[place], relay_s.at[slot], bulk_r.at[place], dest, q_other
-        )
-
-    def relay_one(i, carry):
-        k, way, cs = i // 8, mod(i, 8) // 2, mod(i, 2)
-        dest, copy = second_copy(k, way, cs)
-
-        @pl.when(jnp.logical_not(panel_row(2 * k + cs, dest)))
-        def _():
-            remote(
-                bulk_out.at[0], relay.at[i], bulk_s.at[0], relay_r.at[i], p, q_other
-            ).wait_recv()
-            copy.start()
-        return carry
-
     def panel_row(kk, dest):
         return jnp.logical_and(kk == 0, dest < 4)
 
@@ -310,18 +269,11 @@
         return carry
 
     def fire(n, carry):
-        k, j = n // 16, mod(n, 16)
-        crossing = j < 8
-        dest = jnp.where(crossing, 1 - zh, zh) * 8 + mod(p + j, 8)
-        kk = 2 * k + core
-
-        @pl.when(jnp.logical_not(panel_row(kk, dest)))
-        def _():
-            @pl.when(crossing)
-            def _():
-                first_copy(k, dest).start()
-
-            @pl.when(jnp.logical_and(jnp.logical_not(crossing), dest != p))
+        k, dest = chunk_of(n)
+
+        @pl.when(jnp.logical_not(panel_row(2 * k + core, dest)))
+        def _():
+            @pl.when(dest != p)
             def _():
                 bulk_copy(k, dest).start()
 
@@ -329,6 +281,33 @@
             def _():
                 keep_copy(k).start()
         return carry
+
+    class Beside:
+        def __init__(self, first, fired):
+            self.first, self.fired = first, fired
+
+        def begin(self, b):
+            @pl.when(mod(b, 2) == 0)
+            def _():
+                chunk_copy(self.first + b // 2).wait()
+
+        def work(self, b):
+            n = self.first + b // 2
+            k, dest = chunk_of(n)
+            for i in range(3):
+                m = mod(b, 2) * 3 + i
+                bulk_out[dest * 3 + k, m] = packed(n, 2 * m, 2 * m + 1)
+
+        def end(self, b):
+            n = self.first + b // 2
+
+            @pl.when(mod(b, 2) == 1)
+            def _():
+                next_chunk(n)
+
+                @pl.when(n < self.fired)
+                def _():
+                    fire(n, 0)
 
     lax.fori_loop(0, 4, pack, 0)
     front_load.wait()
@@ -446,14 +425,13 @@
             found.append(jnp.max(jnp.where(hit, ranks, -1), axis=0, keepdims=True))
         return found
 
-    def row_table(i, carry):
-        found = places(jnp.where(i < 6, i * 16 + p, mod(chip, 4)))
+    def row_table(i, carry, block=None):
+        found = places(i * 16 + p if block is None else block)
         for j in range(4):
             first, second = found[2 * j], found[2 * j + 1]
             row_perms[i, j : j + 1, :] = jnp.where(first >= 0, first, second + HALF)
         return carry
 
-    lax.fori_loop(0, 7, row_table, 0)
 
     def col_table(l, carry):
         found = places(l * 8 + q)
@@ -463,9 +441,15 @@
             )
         return carry
 
-    lax.fori_loop(0, 12, col_table, 0)
+    row_table(6, 0, mod(chip, 4))
+
+    def unit_table(slot, carry):
+        m = slot * 2 + chip // 4
+        return col_table(2 * m + 1, col_table(2 * m, carry))
+
+    lax.fori_loop(core, 1 + 2 * core, unit_table, 0)
     lax.fori_loop(first_slot, last_slot, own_unit, 0)
-    lax.fori_loop(4, 16, pack, 0)
+    lax.fori_loop(4, 10, pack, 0)
 
     @pl.when(core == 0)
     def _():
@@ -492,8 +476,7 @@
     for i in range(1, 4):
         dy(i).start()
 
-    lax.fori_loop(0, 16, fire, 0)
-    lax.fori_loop(16, 48, pack, 0)
+    lax.fori_loop(0, 8, fire, 0)
 
     @pl.when(core == 0)
     def _():
@@ -527,6 +510,11 @@
             def _():
                 rows[c] = cols[:, c * 128 : c * 128 + 128, pl.ds(pl.multiple_of(ph * 128, 128), 128)]
 
+
+    lax.fori_loop(10, 16, pack, 0)
+    lax.fori_loop(8, 10, fire, 0)
+    lax.fori_loop(0, 6, row_table, 0)
+    lax.fori_loop(0, 12, col_table, 0)
 
     for i in range(1, 4):
         src = mod(y + i, 4)
@@ -538,8 +526,6 @@
     work[:, 0:SPAN] = 0.5 * (full + full.T)
     work[:, SPAN:] = jnp.zeros((SPAN, SPAN), F32)
 
-    factor_block(0, work, pair)
-
     holder = zl == pl8 // 4
 
     @pl.when(holder)
@@ -551,10 +537,7 @@
             ).wait_recv()
         rz.start()
 
-    lax.fori_loop(16, 24, fire, 0)
-    lax.fori_loop(0, 8, relay_one, 0)
-    lax.fori_loop(24, 32, fire, 0)
-    factor_block(1, work, pair)
+    factor_block(0, work, pair, Beside(16, 18))
 
     @pl.when(jnp.logical_not(holder))
     def _():
@@ -563,12 +546,11 @@
     for i in range(1, 4):
         ry(i).start()
 
-    lax.fori_loop(32, 40, fire, 0)
-    factor_block(2, work, pair)
-    lax.fori_loop(8, 16, relay_one, 0)
-    lax.fori_loop(40, 48, fire, 0)
-    factor_block(3, work, pair)
-    lax.fori_loop(16, 24, relay_one, 0)
+    lax.fori_loop(10, 16, fire, 0)
+    lax.fori_loop(18, 24, fire, 0)
+    factor_block(1, work, pair, Beside(24, 48))
+    factor_block(2, work, pair, Beside(32, 48))
+    factor_block(3, work, pair, Beside(40, 48))
 
     def sent_unit(slot, carry):
         u = slot * 8 + chip
@@ -764,17 +746,6 @@
             return c
 
         lax.fori_loop(0, 6, one, 0)
-
-    def relayed(i, carry):
-        k, way, cs = i // 8, mod(i, 8) // 2, mod(i, 2)
-        dest, copy = second_copy(k, way, cs)
-
-        @pl.when(jnp.logical_not(panel_row(2 * k + cs, dest)))
-        def _():
-            copy.wait_send()
-        return carry
-
-    lax.fori_loop(0, 24, relayed, 0)
 
     def stored(kk, carry):
         store(kk).wait()
@@ -860,8 +831,7 @@
             vmem(768, 256),
             pltpu.VMEM((SPAN, SPAN), BF16),
             pltpu.VMEM((SPAN, SPAN), BF16),
-            vmem(24, 6, HALF, 128),
-            sems(3), sems(2), sems(1), sems(4), sems(1), sems(6), sems(24), sems(24), sems(48), sems(48), sems(24), sems(24),
+            sems(3), sems(2), sems(1), sems(4), sems(1), sems(6), sems(48), sems(48), sems(24), sems(24),
             sems(6), sems(3), sems(24), sems(24), sems(24), sems(1), sems(1), sems(4), sems(4),
             sems(4), sems(1), sems(1), sems(1), sems(4), sems(4),
         ],
@@ -882,7 +852,7 @@
         ],
         out_specs=part,
         scratch_shapes=[pltpu.VMEM((BLOCK, 1024), BF16), pltpu.VMEM((1024, 256), BF16)],
-        compiler_params=pltpu.CompilerParams(vmem_limit_bytes=40 * 2**20),
+        compiler_params=pltpu.CompilerParams(vmem_limit_bytes=60 * 2**20),
     )(row_perms, col_places, front, children)
     return out.reshape(root_front.shape)
 

time: 220 us -> 233 us (1.059)
  the two profiles are of different devices: /device:TPU:85 before, /device:TPU:37 now
where the time goes in v3:
time: 233 us
  Pallas kernels  233 us (100%)
    pallas_call x1, Pallas kernels, body(): pl.pallas_call(kernel, out_shape=[jax.ShapeDtypeStruct(root.shape, F32),...  207 us
    pallas_call x1, Pallas kernels, body(): pl.pallas_call(add_children, grid=(ROW_BLOCKS,), out_shape=jax.ShapeDtype...  26.1 us

profile of v3, /device:TPU:37, one launch (start us, length us, event | category | flops | bytes accessed | tf_op | source)
XLA Modules:
  0.0 232.7 jit_solution(4561702786349175346)
XLA Ops:
  0.0 206.7 %shard_map.37 = (f32[9216,128]{1,0:T(8,128)}, f32[48,6,64,128]{3,2,1,0:T(8,128)}, s32[8,4,128]{2,1,0:T(4,128)}, s32[12,8,128]{2,1,0:T(8,128)}) custom-call(s32[8,6144]{1,0:T(8,128)} %child_map.1, f32[36864,64]{1,0:T(8,128)} %bitcast.3, f32[9216,128]{1,0:T(8,128)} %bitcast.4), custom_call_target="tpu_custom_call" | custom-call | tf_op jit(solution)/shard_map/pallas_call | solution.py:803
  206.7 26.1 %shard_map.38 = f32[9216,128]{1,0:T(8,128)} custom-call(s32[8,4,128]{2,1,0:T(4,128)} %get-tuple-element.9.row_perms, s32[12,8,128]{2,1,0:T(8,128)} %get-tuple-element.10.col_places, f32[9216,128]{1,0:T(8,128)} %get-tuple-element.11.front, f32[48,6,64,128]{3,2,1,0:T(8,128)} %get-tuple-element.12.children), custom_call_target="tpu_custom_call" | custom-call | tf_op jit(solution)/shard_map/pallas_call | solution.py:843

commit v4 on v2

--- a/solution.py
+++ b/solution.py
@@ -49,11 +49,14 @@
     return high, mid, low
 
 
-def factor_128(pair):
+def factor_128(pair, beside):
     lane = lax.broadcasted_iota(jnp.int32, (8, 128), 1)
     sub = lax.broadcasted_iota(jnp.int32, (8, 128), 0)
 
     def step(b, carry):
+        if beside is not None:
+            beside.begin(b)
+            beside.work(b)
         first = pl.multiple_of(b * 8, 8)
         rows = pair[pl.ds(first, 8), :]
         rows_a = rows[:, :128]
@@ -103,12 +106,14 @@
             left, right, (((0,), (0,)), ((), ())), preferred_element_type=F32
         )
         pair[...] = pair[...] - gone
+        if beside is not None:
+            beside.end(b)
         return carry
 
     lax.fori_loop(0, 16, step, 0)
 
 
-def factor_block(jb, work, pair):
+def factor_block(jb, work, pair, beside):
     at = jb * 128
     eye = (
         lax.broadcasted_iota(jnp.int32, (128, 128), 0)
@@ -116,7 +121,7 @@
     ).astype(F32)
     pair[:, 0:128] = work[at : at + 128, at : at + 128]
     pair[:, 128:256] = eye
-    factor_128(pair)
+    factor_128(pair, beside)
     inverse = pair[:, 128:256]
     if jb:
         work[at : at + 128, SPAN : SPAN + at] = dot_full(
@@ -161,9 +166,16 @@
         return pltpu.make_async_copy(src, dst, sem)
 
     def chunk_of(n):
-        k = n // 16
-        late = jnp.where(n < 4, n, 4 + mod(p + n, 12))
-        dest = jnp.where(n < 16, late, mod(p + n, 16))
+        first = jnp.where(
+            ph == 0,
+            jnp.where(n < 12, 8 + mod(p + n, 8), 4 + mod(n, 4)),
+            jnp.where(n < 8, 4 + mod(p + n, 4), 8 + mod(p + n, 8)),
+        )
+        first = jnp.where(n < 4, n, first)
+        late = n - 16
+        k = jnp.where(n < 16, 0, 1 + mod(late // 8, 2))
+        side = jnp.where(n < 32, 1 - ph, ph)
+        dest = jnp.where(n < 16, first, side * 8 + mod(p + n, 8))
         return k, dest
 
     def chunk_copy(n):
@@ -192,6 +204,7 @@
     lax.fori_loop(1, 16, greet_wide, 0)
     for i in range(1, 4):
         greet(p, zl * 4 + mod(y + i, 4))
+
 
     def greet_plane(i, carry):
         greet(i, q_other)
@@ -310,18 +323,17 @@
         return carry
 
     def fire(n, carry):
-        k, j = n // 16, mod(n, 16)
-        crossing = j < 8
-        dest = jnp.where(crossing, 1 - zh, zh) * 8 + mod(p + j, 8)
-        kk = 2 * k + core
-
-        @pl.when(jnp.logical_not(panel_row(kk, dest)))
-        def _():
+        k, dest = chunk_of(n)
+
+        @pl.when(jnp.logical_not(panel_row(2 * k + core, dest)))
+        def _():
+            crossing = dest // 8 != ph
+
             @pl.when(crossing)
             def _():
                 first_copy(k, dest).start()
 
-            @pl.when(jnp.logical_and(jnp.logical_not(crossing), dest != p))
+            @pl.when(jnp.logical_not(jnp.logical_or(crossing, dest == p)))
             def _():
                 bulk_copy(k, dest).start()
 
@@ -329,6 +341,36 @@
             def _():
                 keep_copy(k).start()
         return carry
+
+    def pack_fire(n, carry):
+        return fire(n, pack(n, carry))
+
+    class Beside:
+        def __init__(self, first, fired):
+            self.first, self.fired = first, fired
+
+        def begin(self, b):
+            @pl.when(mod(b, 2) == 0)
+            def _():
+                chunk_copy(self.first + b // 2).wait()
+
+        def work(self, b):
+            n = self.first + b // 2
+            k, dest = chunk_of(n)
+            for i in range(3):
+                m = mod(b, 2) * 3 + i
+                bulk_out[dest * 3 + k, m] = packed(n, 2 * m, 2 * m + 1)
+
+        def end(self, b):
+            n = self.first + b // 2
+
+            @pl.when(mod(b, 2) == 1)
+            def _():
+                next_chunk(n)
+
+                @pl.when(n < self.fired)
+                def _():
+                    fire(n, 0)
 
     lax.fori_loop(0, 4, pack, 0)
     front_load.wait()
@@ -446,14 +488,13 @@
             found.append(jnp.max(jnp.where(hit, ranks, -1), axis=0, keepdims=True))
         return found
 
-    def row_table(i, carry):
-        found = places(jnp.where(i < 6, i * 16 + p, mod(chip, 4)))
+    def row_table(i, carry, block=None):
+        found = places(i * 16 + p if block is None else block)
         for j in range(4):
             first, second = found[2 * j], found[2 * j + 1]
             row_perms[i, j : j + 1, :] = jnp.where(first >= 0, first, second + HALF)
         return carry
 
-    lax.fori_loop(0, 7, row_table, 0)
 
     def col_table(l, carry):
         found = places(l * 8 + q)
@@ -463,9 +504,16 @@
             )
         return carry
 
-    lax.fori_loop(0, 12, col_table, 0)
+    row_table(6, 0, mod(chip, 4))
+
+    def unit_table(slot, carry):
+        m = slot * 2 + chip // 4
+        return col_table(2 * m + 1, col_table(2 * m, carry))
+
+    lax.fori_loop(core, 1 + 2 * core, unit_table, 0)
     lax.fori_loop(first_slot, last_slot, own_unit, 0)
-    lax.fori_loop(4, 16, pack, 0)
+    lax.fori_loop(0, 4, fire, 0)
+    lax.fori_loop(4, 10, pack_fire, 0)
 
     @pl.when(core == 0)
     def _():
@@ -492,8 +540,6 @@
     for i in range(1, 4):
         dy(i).start()
 
-    lax.fori_loop(0, 16, fire, 0)
-    lax.fori_loop(16, 48, pack, 0)
 
     @pl.when(core == 0)
     def _():
@@ -527,6 +573,21 @@
             def _():
                 rows[c] = cols[:, c * 128 : c * 128 + 128, pl.ds(pl.multiple_of(ph * 128, 128), 128)]
 
+
+    lax.fori_loop(10, 20, pack_fire, 0)
+
+    holder = zl == pl8 // 4
+
+    @pl.when(holder)
+    def _():
+        @pl.when(jnp.logical_not(own))
+        def _():
+            remote(
+                rows.at[y], rows.at[y], r1_s.at[0], r1_r.at[0], p, q_other
+            ).wait_recv()
+        rz.start()
+
+    lax.fori_loop(20, 32, pack_fire, 0)
 
     for i in range(1, 4):
         src = mod(y + i, 4)
@@ -538,23 +599,8 @@
     work[:, 0:SPAN] = 0.5 * (full + full.T)
     work[:, SPAN:] = jnp.zeros((SPAN, SPAN), F32)
 
-    factor_block(0, work, pair)
-
-    holder = zl == pl8 // 4
-
-    @pl.when(holder)
-    def _():
-        @pl.when(jnp.logical_not(own))
-        def _():
-            remote(
-                rows.at[y], rows.at[y], r1_s.at[0], r1_r.at[0], p, q_other
-            ).wait_recv()
-        rz.start()
-
-    lax.fori_loop(16, 24, fire, 0)
     lax.fori_loop(0, 8, relay_one, 0)
-    lax.fori_loop(24, 32, fire, 0)
-    factor_block(1, work, pair)
+    factor_block(0, work, pair, Beside(32, 48))
 
     @pl.when(jnp.logical_not(holder))
     def _():
@@ -563,12 +609,13 @@
     for i in range(1, 4):
         ry(i).start()
 
-    lax.fori_loop(32, 40, fire, 0)
-    factor_block(2, work, pair)
     lax.fori_loop(8, 16, relay_one, 0)
-    lax.fori_loop(40, 48, fire, 0)
-    factor_block(3, work, pair)
+    factor_block(1, work, pair, Beside(40, 48))
     lax.fori_loop(16, 24, relay_one, 0)
+    factor_block(2, work, pair, None)
+    factor_block(3, work, pair, None)
+    lax.fori_loop(0, 6, row_table, 0)
+    lax.fori_loop(0, 12, col_table, 0)
 
     def sent_unit(slot, carry):
         u = slot * 8 + chip
@@ -882,7 +929,7 @@
         ],
         out_specs=part,
         scratch_shapes=[pltpu.VMEM((BLOCK, 1024), BF16), pltpu.VMEM((1024, 256), BF16)],
-        compiler_params=pltpu.CompilerParams(vmem_limit_bytes=40 * 2**20),
+        compiler_params=pltpu.CompilerParams(vmem_limit_bytes=60 * 2**20),
     )(row_perms, col_places, front, children)
     return out.reshape(root_front.shape)
 

time: 220 us -> 213 us (0.968)
  the two profiles are of different devices: /device:TPU:85 before, /device:TPU:28 now
where the time goes in v4:
time: 213 us
  Pallas kernels  213 us (100%)
    pallas_call x1, Pallas kernels, body(): pl.pallas_call(kernel, out_shape=[jax.ShapeDtypeStruct(root.shape, F32),...  187 us
    pallas_call x1, Pallas kernels, body(): pl.pallas_call(add_children, grid=(ROW_BLOCKS,), out_shape=jax.ShapeDtype...  26.1 us

profile of v4, /device:TPU:28, one launch (start us, length us, event | category | flops | bytes accessed | tf_op | source)
XLA Modules:
  0.0 213.2 jit_solution(7191568565924803098)
XLA Ops:
  0.0 187.2 %shard_map.37 = (f32[9216,128]{1,0:T(8,128)}, f32[48,6,64,128]{3,2,1,0:T(8,128)}, s32[8,4,128]{2,1,0:T(4,128)}, s32[12,8,128]{2,1,0:T(8,128)}) custom-call(s32[8,6144]{1,0:T(8,128)} %child_map.1, f32[36864,64]{1,0:T(8,128)} %bitcast.3, f32[9216,128]{1,0:T(8,128)} %bitcast.4), custom_call_target="tpu_custom_call" | custom-call | tf_op jit(solution)/shard_map/pallas_call | solution.py:879
  187.2 26.1 %shard_map.38 = f32[9216,128]{1,0:T(8,128)} custom-call(s32[8,4,128]{2,1,0:T(4,128)} %get-tuple-element.9.row_perms, s32[12,8,128]{2,1,0:T(8,128)} %get-tuple-element.10.col_places, f32[9216,128]{1,0:T(8,128)} %get-tuple-element.11.front, f32[48,6,64,128]{3,2,1,0:T(8,128)} %get-tuple-element.12.children), custom_call_target="tpu_custom_call" | custom-call | tf_op jit(solution)/shard_map/pallas_call | solution.py:920

commit v5 on v4

--- a/solution.py
+++ b/solution.py
@@ -140,8 +140,8 @@
 def kernel(
     child_map, child, root, out, bulk_in, row_out, col_out,
     marks, row_perms, col_places, chunk_buf, front, bulk_out, unit_in, front_out, front_in, cols, diag, rows, work,
-    pair, rows_f, rows_h, rows_l, prod, inv_h, inv_l, relay,
-    keep_s, tab_s, s_marks, s_chunk, s_front, s_out, relay_s, relay_r, bulk_s, bulk_r, unit_s, unit_r, front_s, front_r,
+    pair, rows_f, rows_h, rows_l, prod, inv_h, inv_l, relay, kids, pick, wide_buf,
+    kids_s, keep_s, tab_s, s_marks, s_chunk, s_front, s_out, relay_s, relay_r, bulk_s, bulk_r, unit_s, unit_r, front_s, front_r,
     cols_s, cols_r, hand_s, dz_s, dz_r, dy_s, dy_r, r1_s, r1_r, rz_s, rz_r, ry_s, ry_r,
 ):
     p = lax.axis_index("wide")
@@ -416,11 +416,25 @@
     def cols_at(u):
         return cols.at[u // 4, pl.ds(pl.multiple_of(mod(u, 4) * 128, 128), 128), :]
 
-    def cols_copy(u, dc):
+    def cross_copy(u):
         return remote(
-            cols_at(u), cols_at(u), cols_s.at[(u // 8) * 8 + dc], cols_r.at[u],
-            mod(chip + dc, 8) * 2 + core, q,
-        )
+            cols_at(u), cols_at(u), cols_s.at[(u // 8) * 8], cols_r.at[u],
+            mod(chip + 4, 8) * 2 + core, q,
+        )
+
+    def along_copy(u, dx):
+        far = jnp.where(mod(u, 8) == chip, 0, 3)
+        return remote(
+            cols_at(u), cols_at(u), cols_s.at[(u // 8) * 8 + far + dx], cols_r.at[u],
+            (ph * 4 + mod(chip + dx, 4)) * 2 + core, q,
+        )
+
+    def along(u):
+        def send(dx, c):
+            along_copy(u, dx).start()
+            return c
+
+        lax.fori_loop(1, 4, send, 0)
 
     def hand_copy(u):
         return remote(cols_at(u), cols_at(u), hand_s.at[u], cols_r.at[u], chip * 2 + 1 - core, q)
@@ -451,18 +465,22 @@
             jnp.concatenate(sides, axis=1) + front_in[slot]
         )
 
-        def send(dc, c):
-            cols_copy(u, dc).start()
-            return c
-
-        lax.fori_loop(1, 8, send, 0)
+        cross_copy(u).start()
+        along(u)
         hand_copy(u).start()
         return carry
 
+    def spread_on(slot, carry):
+        u = slot * 8 + mod(chip + 4, 8)
+        cross_copy(u).wait_recv()
+        along(u)
+        hand_copy(u).start()
+        return carry
+
     def hand_on(u, carry):
-        @pl.when(mod(u, 8) != chip)
-        def _():
-            cols_copy(u, 1).wait_recv()
+        @pl.when(mod(u - chip + 32, 4) != 0)
+        def _():
+            cross_copy(u).wait_recv()
             hand_copy(u).start()
         return carry
 
@@ -513,7 +531,9 @@
     lax.fori_loop(core, 1 + 2 * core, unit_table, 0)
     lax.fori_loop(first_slot, last_slot, own_unit, 0)
     lax.fori_loop(0, 4, fire, 0)
-    lax.fori_loop(4, 10, pack_fire, 0)
+    lax.fori_loop(4, 8, pack_fire, 0)
+    lax.fori_loop(first_slot, last_slot, spread_on, 0)
+    lax.fori_loop(8, 10, pack_fire, 0)
 
     @pl.when(core == 0)
     def _():
@@ -620,11 +640,14 @@
     def sent_unit(slot, carry):
         u = slot * 8 + chip
 
-        def one(dc, c):
-            cols_copy(u, dc).wait_send()
+        cross_copy(u).wait_send()
+
+        def one(dx, c):
+            along_copy(u, dx).wait_send()
+            along_copy(slot * 8 + mod(chip + 4, 8), dx).wait_send()
             return c
 
-        lax.fori_loop(1, 8, one, 0)
+        lax.fori_loop(1, 4, one, 0)
         hand_copy(u).wait_send()
         return carry
 
@@ -748,28 +771,51 @@
             )
             front[pl.ds(0, BLOCK, stride=COL_BLOCKS), :] = jnp.where(lower, tile, tile.T)
 
-    lax.fori_loop(0, 6, lambda kk, c: (store(kk).start(), c)[1], 0)
-
-    def landed(i, carry):
-        kk, g = i // 8, mod(i, 8)
-        mine = jnp.logical_and(g == chip, mod(kk, 2) == core)
-
-        @pl.when(jnp.logical_not(jnp.logical_or(mine, panel_row(kk, p))))
-        def _():
-            remote(
-                bulk_out.at[0], bulk_in.at[i], bulk_s.at[0], bulk_r.at[i], g * 2 + mod(kk, 2), q
-            ).wait_recv()
-        return carry
-
-    lax.fori_loop(0, 48, landed, 0)
-
-    def kept(k, carry):
-        @pl.when(jnp.logical_not(panel_row(2 * k + core, p)))
-        def _():
-            keep_copy(k).wait()
-        return carry
-
-    lax.fori_loop(0, 3, kept, 0)
+    def arrived(kk):
+        def landed(g, c):
+            mine = jnp.logical_and(g == chip, mod(kk, 2) == core)
+
+            @pl.when(jnp.logical_not(mine))
+            def _():
+                remote(
+                    bulk_out.at[0], bulk_in.at[kk * 8 + g], bulk_s.at[0], bulk_r.at[kk * 8 + g],
+                    g * 2 + mod(kk, 2), q,
+                ).wait_recv()
+
+            @pl.when(mine)
+            def _():
+                keep_copy(kk // 2).wait()
+            return c
+
+        lax.fori_loop(0, 8, landed, 0)
+
+    def early(kk, carry):
+        @pl.when(jnp.logical_not(panel_row(kk, p)))
+        def _():
+            arrived(kk)
+            at = pl.multiple_of(kk * 8, 8)
+            load = local(bulk_in.at[pl.ds(at, 8)], kids, kids_s.at[0])
+            load.start()
+            set_pick(pick, row_perms, kk)
+            load.wait()
+
+            def one(m, c):
+                total = add_pair(m, col_places, lambda g: kids[g, m], pick, wide_buf)
+                for h in range(2):
+                    where = pl.ds(kk * (128 * COL_BLOCKS) + 2 * m + h, BLOCK, stride=COL_BLOCKS)
+                    side = total[:, h * 128 : h * 128 + 128]
+                    if h == 0:
+                        side = jnp.where(jnp.logical_and(m == 0, q < 4), 0.0, side)
+                    front[where, :] = front[where, :] + side
+                return c
+
+            lax.fori_loop(0, 6, one, 0)
+        store(kk).start()
+        return carry
+
+    lax.fori_loop(EARLY, 6, lambda kk, c: (store(kk).start(), c)[1], 0)
+    lax.fori_loop(0, EARLY, early, 0)
+    lax.fori_loop(EARLY, 6, lambda kk, c: (arrived(kk), c)[1], 0)
     tables = [
         local(row_perms, row_out, tab_s.at[0]), local(col_places, col_out, tab_s.at[1])
     ]
@@ -830,36 +876,45 @@
     lax.fori_loop(0, 6, stored, 0)
 
 
+def set_pick(pick, row_perms, kk):
+    level = lax.broadcasted_iota(jnp.int32, (128, 128), 1)
+    for j in range(4):
+        order = jnp.broadcast_to(row_perms[kk, j : j + 1, :], (128, 128)).T
+        table = jnp.where(order == level, 1.0, 0.0).astype(BF16)
+        pick[:, j * 128 : j * 128 + 128] = table
+        pick[:, 512 + j * 128 : 640 + j * 128] = table
+
+
+def add_pair(m, col_places, child_of, pick, wide_buf):
+    for g in range(CHILDREN):
+        for h in range(2):
+            place = jnp.broadcast_to(col_places[2 * m + h, g : g + 1, :], (HALF, 128))
+            taken = jnp.take_along_axis(
+                child_of(g), jnp.maximum(place, 0), axis=1, mode="promise_in_bounds"
+            )
+            high, low = halves(jnp.where(place >= 0, taken, 0.0))
+            wide_buf[g * 64 : g * 64 + 64, h * 128 : h * 128 + 128] = high
+            wide_buf[512 + g * 64 : 576 + g * 64, h * 128 : h * 128 + 128] = low
+    return jnp.dot(pick[...], wide_buf[...], preferred_element_type=F32)
+
+
+EARLY = 4
+
+
 def add_children(row_perms, col_places, front, children, out, pick, wide_buf):
-    kk = pl.program_id(0)
-    p = lax.axis_index("wide")
+    kk = mod(pl.program_id(0) + EARLY, ROW_BLOCKS)
     q = lax.axis_index("narrow")
-    panel = jnp.logical_and(kk == 0, p < 4)
-
-    @pl.when(panel)
+
+    @pl.when(kk < EARLY)
     def _():
         out[...] = front[...]
 
-    @pl.when(jnp.logical_not(panel))
-    def _():
-        level = lax.broadcasted_iota(jnp.int32, (128, 128), 1)
-        for j in range(4):
-            order = jnp.broadcast_to(row_perms[kk, j : j + 1, :], (128, 128)).T
-            table = jnp.where(order == level, 1.0, 0.0).astype(BF16)
-            pick[:, j * 128 : j * 128 + 128] = table
-            pick[:, 512 + j * 128 : 640 + j * 128] = table
+    @pl.when(kk >= EARLY)
+    def _():
+        set_pick(pick, row_perms, kk)
 
         def one(m, carry):
-            for g in range(CHILDREN):
-                for h in range(2):
-                    place = jnp.broadcast_to(col_places[2 * m + h, g : g + 1, :], (HALF, 128))
-                    taken = jnp.take_along_axis(
-                        children[g, m], jnp.maximum(place, 0), axis=1, mode="promise_in_bounds"
-                    )
-                    high, low = halves(jnp.where(place >= 0, taken, 0.0))
-                    wide_buf[g * 64 : g * 64 + 64, h * 128 : h * 128 + 128] = high
-                    wide_buf[512 + g * 64 : 576 + g * 64, h * 128 : h * 128 + 128] = low
-            total = jnp.dot(pick[...], wide_buf[...], preferred_element_type=F32)
+            total = add_pair(m, col_places, lambda g: children[g, m], pick, wide_buf)
             for h in range(2):
                 where = pl.ds(2 * m + h, BLOCK, stride=COL_BLOCKS)
                 side = total[:, h * 128 : h * 128 + 128]
@@ -908,7 +963,10 @@
             pltpu.VMEM((SPAN, SPAN), BF16),
             pltpu.VMEM((SPAN, SPAN), BF16),
             vmem(24, 6, HALF, 128),
-            sems(3), sems(2), sems(1), sems(4), sems(1), sems(6), sems(24), sems(24), sems(48), sems(48), sems(24), sems(24),
+            vmem(CHILDREN, 6, HALF, 128),
+            pltpu.VMEM((BLOCK, 1024), BF16),
+            pltpu.VMEM((1024, 256), BF16),
+            sems(1), sems(3), sems(2), sems(1), sems(4), sems(1), sems(6), sems(24), sems(24), sems(48), sems(48), sems(24), sems(24),
             sems(6), sems(3), sems(24), sems(24), sems(24), sems(1), sems(1), sems(4), sems(4),
             sems(4), sems(1), sems(1), sems(1), sems(4), sems(4),
         ],
@@ -916,7 +974,7 @@
             collective_id=0, has_side_effects=True, vmem_limit_bytes=60 * 2**20
         ),
     )(child_map, child, root)
-    part = pl.BlockSpec((BLOCK * COL_BLOCKS, BLOCK), lambda i: (i, 0))
+    part = pl.BlockSpec((BLOCK * COL_BLOCKS, BLOCK), lambda i: (mod(i + EARLY, ROW_BLOCKS), 0))
     out = pl.pallas_call(
         add_children,
         grid=(ROW_BLOCKS,),
@@ -925,7 +983,10 @@
             pl.BlockSpec((8, 4, 128), lambda i: (0, 0, 0)),
             pl.BlockSpec((COL_BLOCKS, CHILDREN, 128), lambda i: (0, 0, 0)),
             part,
-            pl.BlockSpec((CHILDREN, 6, HALF, 128), lambda i: (i, 0, 0, 0)),
+            pl.BlockSpec(
+                (CHILDREN, 6, HALF, 128),
+                lambda i: (jnp.minimum(i + EARLY, ROW_BLOCKS - 1), 0, 0, 0),
+            ),
         ],
         out_specs=part,
         scratch_shapes=[pltpu.VMEM((BLOCK, 1024), BF16), pltpu.VMEM((1024, 256), BF16)],

time: 213 us -> 205 us (0.962)
  the two profiles are of different devices: /device:TPU:28 before, /device:TPU:85 now
where the time goes in v5:
time: 205 us; the launch traced here: 202 us
  Pallas kernels  202 us (99%)
    pallas_call x1, Pallas kernels, body(): pl.pallas_call(kernel, out_shape=[jax.ShapeDtypeStruct(root.shape, F32),...  188 us
    pallas_call x1, Pallas kernels, body(): pl.pallas_call(add_children, grid=(ROW_BLOCKS,), out_shape=jax.ShapeDtype...  14 us

profile of v5, /device:TPU:85, one launch (start us, length us, event | category | flops | bytes accessed | tf_op | source)
XLA Modules:
  0.0 201.9 jit_solution(17546171247268833270)
XLA Ops:
  0.0 187.9 %shard_map.37 = (f32[9216,128]{1,0:T(8,128)}, f32[48,6,64,128]{3,2,1,0:T(8,128)}, s32[8,4,128]{2,1,0:T(4,128)}, s32[12,8,128]{2,1,0:T(8,128)}) custom-call(s32[8,6144]{1,0:T(8,128)} %child_map.1, f32[36864,64]{1,0:T(8,128)} %bitcast.3, f32[9216,128]{1,0:T(8,128)} %bitcast.4), custom_call_target="tpu_custom_call" | custom-call | tf_op jit(solution)/shard_map/pallas_call | solution.py:934
  187.9 14.0 %shard_map.38 = f32[9216,128]{1,0:T(8,128)} custom-call(s32[8,4,128]{2,1,0:T(4,128)} %get-tuple-element.9.row_perms, s32[12,8,128]{2,1,0:T(8,128)} %get-tuple-element.10.col_places, f32[9216,128]{1,0:T(8,128)} %get-tuple-element.11.front, f32[48,6,64,128]{3,2,1,0:T(8,128)} %get-tuple-element.12.children), custom_call_target="tpu_custom_call" | custom-call | tf_op jit(solution)/shard_map/pallas_call | solution.py:978

commit v6 on v5

--- a/solution.py
+++ b/solution.py
@@ -524,6 +524,17 @@
 
     row_table(6, 0, mod(chip, 4))
 
+    class Tables:
+        def begin(self, b):
+            pass
+
+        def work(self, b):
+            col_table(jnp.minimum(b, 11), 0)
+            row_table(jnp.minimum(b, 5), 0)
+
+        def end(self, b):
+            pass
+
     def unit_table(slot, carry):
         m = slot * 2 + chip // 4
         return col_table(2 * m + 1, col_table(2 * m, carry))
@@ -607,7 +618,7 @@
             ).wait_recv()
         rz.start()
 
-    lax.fori_loop(20, 32, pack_fire, 0)
+    lax.fori_loop(20, 24, pack_fire, 0)
 
     for i in range(1, 4):
         src = mod(y + i, 4)
@@ -620,7 +631,7 @@
     work[:, SPAN:] = jnp.zeros((SPAN, SPAN), F32)
 
     lax.fori_loop(0, 8, relay_one, 0)
-    factor_block(0, work, pair, Beside(32, 48))
+    factor_block(0, work, pair, Beside(24, 48))
 
     @pl.when(jnp.logical_not(holder))
     def _():
@@ -630,12 +641,10 @@
         ry(i).start()
 
     lax.fori_loop(8, 16, relay_one, 0)
-    factor_block(1, work, pair, Beside(40, 48))
+    factor_block(1, work, pair, Beside(32, 48))
     lax.fori_loop(16, 24, relay_one, 0)
-    factor_block(2, work, pair, None)
-    factor_block(3, work, pair, None)
-    lax.fori_loop(0, 6, row_table, 0)
-    lax.fori_loop(0, 12, col_table, 0)
+    factor_block(2, work, pair, Beside(40, 48))
+    factor_block(3, work, pair, Tables())
 
     def sent_unit(slot, carry):
         u = slot * 8 + chip
@@ -703,18 +712,20 @@
         total += jnp.dot(inv_l[...], high, preferred_element_type=F32)
         return total
 
-    def solve_rows(kk, carry):
-        block = jnp.concatenate([rows[c, kk] for c in range(4)], axis=0)
-        turned = solve(block).T
-        at = pl.multiple_of(kk * 128, 128)
+    def solve_rows(i, carry):
+        parts = [
+            jnp.concatenate([rows[c, 2 * i + h] for c in range(4)], axis=0) for h in range(2)
+        ]
+        turned = solve(jnp.concatenate(parts, axis=1)).T
+        at = pl.multiple_of(i * 256, 256)
         high, low = halves(turned)
-        rows_h[pl.ds(at, 128), :] = high
-        rows_l[pl.ds(at, 128), :] = low
+        rows_h[pl.ds(at, 256), :] = high
+        rows_l[pl.ds(at, 256), :] = low
         for c in range(4):
-            rows_f[c, pl.ds(at, 128), :] = turned[:, c * 128 : c * 128 + 128]
-        return carry
-
-    lax.fori_loop(0, 6, solve_rows, 0)
+            rows_f[c, pl.ds(at, 256), :] = turned[:, c * 128 : c * 128 + 128]
+        return carry
+
+    lax.fori_loop(0, 3, solve_rows, 0)
 
     def solve_cols(m, carry):
         solved = solve(cols[m])

time: 205 us -> 212 us (1.034); the launches traced: 202 us -> 212 us
  Pallas kernels: 202 us -> 212 us
    pallas_call x1, Pallas kernels: 188 us -> 198 us  [body(): pl.pallas_call(kernel, out_shape=[jax.ShapeDtypeStruct(root.shape, F32),...]
where the time goes in v6:
time: 212 us
  Pallas kernels  212 us (100%)
    pallas_call x1, Pallas kernels, body(): pl.pallas_call(kernel, out_shape=[jax.ShapeDtypeStruct(root.shape, F32),...  198 us
    pallas_call x1, Pallas kernels, body(): pl.pallas_call(add_children, grid=(ROW_BLOCKS,), out_shape=jax.ShapeDtype...  14 us

profile of v6, /device:TPU:85, one launch (start us, length us, event | category | flops | bytes accessed | tf_op | source)
XLA Modules:
  0.0 211.7 jit_solution(16328143630584593006)
XLA Ops:
  0.0 197.7 %shard_map.37 = (f32[9216,128]{1,0:T(8,128)}, f32[48,6,64,128]{3,2,1,0:T(8,128)}, s32[8,4,128]{2,1,0:T(4,128)}, s32[12,8,128]{2,1,0:T(8,128)}) custom-call(s32[8,6144]{1,0:T(8,128)} %child_map.1, f32[36864,64]{1,0:T(8,128)} %bitcast.3, f32[9216,128]{1,0:T(8,128)} %bitcast.4), custom_call_target="tpu_custom_call" | custom-call | tf_op jit(solution)/shard_map/pallas_call | solution.py:945
  197.7 14.0 %shard_map.38 = f32[9216,128]{1,0:T(8,128)} custom-call(s32[8,4,128]{2,1,0:T(4,128)} %get-tuple-element.9.row_perms, s32[12,8,128]{2,1,0:T(8,128)} %get-tuple-element.10.col_places, f32[9216,128]{1,0:T(8,128)} %get-tuple-element.11.front, f32[48,6,64,128]{3,2,1,0:T(8,128)} %get-tuple-element.12.children), custom_call_target="tpu_custom_call" | custom-call | tf_op jit(solution)/shard_map/pallas_call | solution.py:989

commit v7 on v6

--- a/solution.py
+++ b/solution.py
@@ -49,55 +49,82 @@
     return high, mid, low
 
 
+def factor_eight(cols):
+    e = {}
+    for a in range(8):
+        for j in range(a + 1):
+            e[a, j] = jnp.broadcast_to(cols[j][a : a + 1, :], (8, 128))
+    inv = []
+    low = {}
+    for j in range(8):
+        d = e[j, j]
+        r = lax.rsqrt(d)
+        r = r * (1.5 - 0.5 * d * r * r)
+        inv.append(r)
+        for a in range(j + 1, 8):
+            low[a, j] = e[a, j] * r
+        for a in range(j + 1, 8):
+            for c in range(j + 1, a + 1):
+                e[a, c] = e[a, c] - low[a, j] * low[c, j]
+    return low, inv
+
+
+def solve_eight(rows, low, inv):
+    found = []
+    for a in range(8):
+        row = jnp.broadcast_to(rows[a : a + 1, :], (8, 128))
+        for j in range(a):
+            row = row - low[a, j] * found[j]
+        found.append(row * inv[a])
+    return found
+
+
 def factor_128(pair, beside):
-    lane = lax.broadcasted_iota(jnp.int32, (8, 128), 1)
+    lane = lax.broadcasted_iota(jnp.int32, (16, 128), 1)
     sub = lax.broadcasted_iota(jnp.int32, (8, 128), 0)
+
+    def spread(value, j):
+        return jnp.broadcast_to(value[:, j : j + 1], (8, 128))
+
+    def gather_rows(found):
+        total = found[0]
+        for a in range(1, 8):
+            total = jnp.where(sub == a, found[a], total)
+        return total
 
     def step(b, carry):
         if beside is not None:
             beside.begin(b)
             beside.work(b)
-        first = pl.multiple_of(b * 8, 8)
-        rows = pair[pl.ds(first, 8), :]
-        rows_a = rows[:, :128]
-        rows_b = rows[:, 128:]
-        turned = pltpu.roll(rows_a, mod(128 - first, 128), 1)
-        cols = [jnp.broadcast_to(turned[:, j : j + 1], (8, 128)) for j in range(8)]
-        e = {}
+        first = pl.multiple_of(b * 16, 16)
+        rows = pair[pl.ds(first, 16), :]
+        back = mod(128 - first, 128)
+        top_a, top_b = rows[0:8, :128], rows[0:8, 128:]
+        end_a, end_b = rows[8:16, :128], rows[8:16, 128:]
+        top_t = pltpu.roll(top_a, back, 1)
+        end_t = pltpu.roll(end_a, back, 1)
+        low, inv = factor_eight([spread(top_t, j) for j in range(8)])
+        ups_t = solve_eight(top_t, low, inv)
+        ups_a = solve_eight(top_a, low, inv)
+        ups_b = solve_eight(top_b, low, inv)
+        link = []
         for a in range(8):
-            for j in range(a + 1):
-                e[a, j] = jnp.broadcast_to(cols[j][a : a + 1, :], (8, 128))
-        inv = []
-        low = {}
-        for j in range(8):
-            d = e[j, j]
-            r = lax.rsqrt(d)
-            r = r * (1.5 - 0.5 * d * r * r)
-            inv.append(r)
-            for a in range(j + 1, 8):
-                low[a, j] = e[a, j] * r
-            for a in range(j + 1, 8):
-                for c in range(j + 1, a + 1):
-                    e[a, c] = e[a, c] - low[a, j] * low[c, j]
-        ups_a = []
-        ups_b = []
-        out_a = jnp.zeros((8, 128), F32)
-        out_b = jnp.zeros((8, 128), F32)
+            value = spread(end_t, a)
+            for j in range(a):
+                value = value - link[j] * low[a, j]
+            link.append(value * inv[a])
         for a in range(8):
-            row_a = jnp.broadcast_to(rows_a[a : a + 1, :], (8, 128))
-            row_b = jnp.broadcast_to(rows_b[a : a + 1, :], (8, 128))
-            for j in range(a):
-                row_a = row_a - low[a, j] * ups_a[j]
-                row_b = row_b - low[a, j] * ups_b[j]
-            row_a = row_a * inv[a]
-            row_b = row_b * inv[a]
-            ups_a.append(row_a)
-            ups_b.append(row_b)
-            out_a = jnp.where(sub == a, row_a, out_a)
-            out_b = jnp.where(sub == a, row_b, out_b)
-        done = jnp.concatenate([out_a, out_b], axis=1)
-        pair[pl.ds(first, 8), :] = done
-        mult = jnp.where(lane >= first + 8, out_a, 0.0)
+            end_t = end_t - link[a] * ups_t[a]
+            end_a = end_a - link[a] * ups_a[a]
+            end_b = end_b - link[a] * ups_b[a]
+        low, inv = factor_eight([spread(end_t, 8 + j) for j in range(8)])
+        more_a = solve_eight(end_a, low, inv)
+        more_b = solve_eight(end_b, low, inv)
+        done_a = jnp.concatenate([gather_rows(ups_a), gather_rows(more_a)], axis=0)
+        done_b = jnp.concatenate([gather_rows(ups_b), gather_rows(more_b)], axis=0)
+        done = jnp.concatenate([done_a, done_b], axis=1)
+        pair[pl.ds(first, 16), :] = done
+        mult = jnp.where(lane >= first + 16, done_a, 0.0)
         mh, mm, ml = thirds(mult)
         uh, um, ul = thirds(done)
         left = jnp.concatenate([mh, mh, mm, mh, ml, mm], axis=0).astype(BF16)
@@ -110,7 +137,7 @@
             beside.end(b)
         return carry
 
-    lax.fori_loop(0, 16, step, 0)
+    lax.fori_loop(0, 8, step, 0)
 
 
 def factor_block(jb, work, pair, beside):
@@ -346,31 +373,21 @@
         return fire(n, pack(n, carry))
 
     class Beside:
-        def __init__(self, first, fired):
-            self.first, self.fired = first, fired
+        def __init__(self, first):
+            self.first = first
 
         def begin(self, b):
-            @pl.when(mod(b, 2) == 0)
-            def _():
-                chunk_copy(self.first + b // 2).wait()
+            chunk_copy(self.first + b).wait()
 
         def work(self, b):
-            n = self.first + b // 2
+            n = self.first + b
             k, dest = chunk_of(n)
-            for i in range(3):
-                m = mod(b, 2) * 3 + i
+            for m in range(6):
                 bulk_out[dest * 3 + k, m] = packed(n, 2 * m, 2 * m + 1)
 
         def end(self, b):
-            n = self.first + b // 2
-
-            @pl.when(mod(b, 2) == 1)
-            def _():
-                next_chunk(n)
-
-                @pl.when(n < self.fired)
-                def _():
-                    fire(n, 0)
+            next_chunk(self.first + b)
+            fire(self.first + b, 0)
 
     lax.fori_loop(0, 4, pack, 0)
     front_load.wait()
@@ -529,7 +546,8 @@
             pass
 
         def work(self, b):
-            col_table(jnp.minimum(b, 11), 0)
+            col_table(jnp.minimum(2 * b, 11), 0)
+            col_table(jnp.minimum(2 * b + 1, 11), 0)
             row_table(jnp.minimum(b, 5), 0)
 
         def end(self, b):
@@ -618,7 +636,7 @@
             ).wait_recv()
         rz.start()
 
-    lax.fori_loop(20, 24, pack_fire, 0)
+    lax.fori_loop(20, 32, pack_fire, 0)
 
     for i in range(1, 4):
         src = mod(y + i, 4)
@@ -631,7 +649,7 @@
     work[:, SPAN:] = jnp.zeros((SPAN, SPAN), F32)
 
     lax.fori_loop(0, 8, relay_one, 0)
-    factor_block(0, work, pair, Beside(24, 48))
+    factor_block(0, work, pair, Beside(32))
 
     @pl.when(jnp.logical_not(holder))
     def _():
@@ -641,9 +659,9 @@
         ry(i).start()
 
     lax.fori_loop(8, 16, relay_one, 0)
-    factor_block(1, work, pair, Beside(32, 48))
+    factor_block(1, work, pair, Beside(40))
     lax.fori_loop(16, 24, relay_one, 0)
-    factor_block(2, work, pair, Beside(40, 48))
+    factor_block(2, work, pair, None)
     factor_block(3, work, pair, Tables())
 
     def sent_unit(slot, carry):

time: 212 us -> 192 us (0.906)
  Pallas kernels: 212 us -> 191 us
    pallas_call x1, Pallas kernels: 198 us -> 177 us  [body(): pl.pallas_call(kernel, out_shape=[jax.ShapeDtypeStruct(root.shape, F32),...]
where the time goes in v7:
time: 192 us; the launch traced here: 191 us
  Pallas kernels  191 us (99%)
    pallas_call x1, Pallas kernels, body(): pl.pallas_call(kernel, out_shape=[jax.ShapeDtypeStruct(root.shape, F32),...  177 us
    pallas_call x1, Pallas kernels, body(): pl.pallas_call(add_children, grid=(ROW_BLOCKS,), out_shape=jax.ShapeDtype...  14 us

profile of v7, /device:TPU:85, one launch (start us, length us, event | category | flops | bytes accessed | tf_op | source)
XLA Modules:
  0.0 191.0 jit_solution(1925163357051521021)
XLA Ops:
  0.0 177.0 %shard_map.37 = (f32[9216,128]{1,0:T(8,128)}, f32[48,6,64,128]{3,2,1,0:T(8,128)}, s32[8,4,128]{2,1,0:T(4,128)}, s32[12,8,128]{2,1,0:T(8,128)}) custom-call(s32[8,6144]{1,0:T(8,128)} %child_map.1, f32[36864,64]{1,0:T(8,128)} %bitcast.3, f32[9216,128]{1,0:T(8,128)} %bitcast.4), custom_call_target="tpu_custom_call" | custom-call | tf_op jit(solution)/shard_map/pallas_call | solution.py:963
  177.0 14.0 %shard_map.38 = f32[9216,128]{1,0:T(8,128)} custom-call(s32[8,4,128]{2,1,0:T(4,128)} %get-tuple-element.9.row_perms, s32[12,8,128]{2,1,0:T(8,128)} %get-tuple-element.10.col_places, f32[9216,128]{1,0:T(8,128)} %get-tuple-element.11.front, f32[48,6,64,128]{3,2,1,0:T(8,128)} %get-tuple-element.12.children), custom_call_target="tpu_custom_call" | custom-call | tf_op jit(solution)/shard_map/pallas_call | solution.py:1007

commit v8 on v7

--- a/solution.py
+++ b/solution.py
@@ -637,6 +637,7 @@
         rz.start()
 
     lax.fori_loop(20, 32, pack_fire, 0)
+    lax.fori_loop(0, 8, relay_one, 0)
 
     for i in range(1, 4):
         src = mod(y + i, 4)
@@ -648,7 +649,7 @@
     work[:, 0:SPAN] = 0.5 * (full + full.T)
     work[:, SPAN:] = jnp.zeros((SPAN, SPAN), F32)
 
-    lax.fori_loop(0, 8, relay_one, 0)
+    lax.fori_loop(8, 16, relay_one, 0)
     factor_block(0, work, pair, Beside(32))
 
     @pl.when(jnp.logical_not(holder))
@@ -658,9 +659,8 @@
     for i in range(1, 4):
         ry(i).start()
 
-    lax.fori_loop(8, 16, relay_one, 0)
+    lax.fori_loop(16, 24, relay_one, 0)
     factor_block(1, work, pair, Beside(40))
-    lax.fori_loop(16, 24, relay_one, 0)
     factor_block(2, work, pair, None)
     factor_block(3, work, pair, Tables())
 

time: 192 us -> 202 us (1.052)
  Pallas kernels: 191 us -> 202 us
    pallas_call x1, Pallas kernels: 177 us -> 188 us  [body(): pl.pallas_call(kernel, out_shape=[jax.ShapeDtypeStruct(root.shape, F32),...]
where the time goes in v8:
time: 202 us
  Pallas kernels  202 us (100%)
    pallas_call x1, Pallas kernels, body(): pl.pallas_call(kernel, out_shape=[jax.ShapeDtypeStruct(root.shape, F32),...  188 us
    pallas_call x1, Pallas kernels, body(): pl.pallas_call(add_children, grid=(ROW_BLOCKS,), out_shape=jax.ShapeDtype...  14 us

profile of v8, /device:TPU:85, one launch (start us, length us, event | category | flops | bytes accessed | tf_op | source)
XLA Modules:
  0.0 202.1 jit_solution(12041008442398903970)
XLA Ops:
  0.0 188.1 %shard_map.37 = (f32[9216,128]{1,0:T(8,128)}, f32[48,6,64,128]{3,2,1,0:T(8,128)}, s32[8,4,128]{2,1,0:T(4,128)}, s32[12,8,128]{2,1,0:T(8,128)}) custom-call(s32[8,6144]{1,0:T(8,128)} %child_map.1, f32[36864,64]{1,0:T(8,128)} %bitcast.3, f32[9216,128]{1,0:T(8,128)} %bitcast.4), custom_call_target="tpu_custom_call" | custom-call | tf_op jit(solution)/shard_map/pallas_call | solution.py:963
  188.1 14.0 %shard_map.38 = f32[9216,128]{1,0:T(8,128)} custom-call(s32[8,4,128]{2,1,0:T(4,128)} %get-tuple-element.9.row_perms, s32[12,8,128]{2,1,0:T(8,128)} %get-tuple-element.10.col_places, f32[9216,128]{1,0:T(8,128)} %get-tuple-element.11.front, f32[48,6,64,128]{3,2,1,0:T(8,128)} %get-tuple-element.12.children), custom_call_target="tpu_custom_call" | custom-call | tf_op jit(solution)/shard_map/pallas_call | solution.py:1007

commit v9 on v7

--- a/solution.py
+++ b/solution.py
@@ -559,10 +559,9 @@
 
     lax.fori_loop(core, 1 + 2 * core, unit_table, 0)
     lax.fori_loop(first_slot, last_slot, own_unit, 0)
-    lax.fori_loop(0, 4, fire, 0)
-    lax.fori_loop(4, 8, pack_fire, 0)
+    lax.fori_loop(4, 8, pack, 0)
     lax.fori_loop(first_slot, last_slot, spread_on, 0)
-    lax.fori_loop(8, 10, pack_fire, 0)
+    lax.fori_loop(8, 10, pack, 0)
 
     @pl.when(core == 0)
     def _():
@@ -623,7 +622,8 @@
                 rows[c] = cols[:, c * 128 : c * 128 + 128, pl.ds(pl.multiple_of(ph * 128, 128), 128)]
 
 
-    lax.fori_loop(10, 20, pack_fire, 0)
+    lax.fori_loop(0, 8, fire, 0)
+    lax.fori_loop(10, 20, pack, 0)
 
     holder = zl == pl8 // 4
 
@@ -636,7 +636,18 @@
             ).wait_recv()
         rz.start()
 
-    lax.fori_loop(20, 32, pack_fire, 0)
+    lax.fori_loop(8, 12, fire, 0)
+    lax.fori_loop(20, 26, pack, 0)
+
+    @pl.when(jnp.logical_not(holder))
+    def _():
+        rz.wait_recv()
+
+    for i in range(1, 4):
+        ry(i).start()
+
+    lax.fori_loop(12, 26, fire, 0)
+    lax.fori_loop(26, 32, pack_fire, 0)
 
     for i in range(1, 4):
         src = mod(y + i, 4)
@@ -650,13 +661,6 @@
 
     lax.fori_loop(0, 8, relay_one, 0)
     factor_block(0, work, pair, Beside(32))
-
-    @pl.when(jnp.logical_not(holder))
-    def _():
-        rz.wait_recv()
-
-    for i in range(1, 4):
-        ry(i).start()
 
     lax.fori_loop(8, 16, relay_one, 0)
     factor_block(1, work, pair, Beside(40))

time: 192 us -> 220 us (1.15)
  the two profiles are of different devices: /device:TPU:85 before, /device:TPU:31 now
where the time goes in v9:
time: 220 us; the launch traced here: 219 us
  Pallas kernels  219 us (100%)
    pallas_call x1, Pallas kernels, body(): pl.pallas_call(kernel, out_shape=[jax.ShapeDtypeStruct(root.shape, F32),...  205 us
    pallas_call x1, Pallas kernels, body(): pl.pallas_call(add_children, grid=(ROW_BLOCKS,), out_shape=jax.ShapeDtype...  14 us

profile of v9, /device:TPU:31, one launch (start us, length us, event | category | flops | bytes accessed | tf_op | source)
XLA Modules:
  0.0 219.3 jit_solution(16649169094577311047)
XLA Ops:
  0.0 205.3 %shard_map.37 = (f32[9216,128]{1,0:T(8,128)}, f32[48,6,64,128]{3,2,1,0:T(8,128)}, s32[8,4,128]{2,1,0:T(4,128)}, s32[12,8,128]{2,1,0:T(8,128)}) custom-call(s32[8,6144]{1,0:T(8,128)} %child_map.1, f32[36864,64]{1,0:T(8,128)} %bitcast.3, f32[9216,128]{1,0:T(8,128)} %bitcast.4), custom_call_target="tpu_custom_call" | custom-call | tf_op jit(solution)/shard_map/pallas_call | solution.py:967
  205.3 14.0 %shard_map.38 = f32[9216,128]{1,0:T(8,128)} custom-call(s32[8,4,128]{2,1,0:T(4,128)} %get-tuple-element.9.row_perms, s32[12,8,128]{2,1,0:T(8,128)} %get-tuple-element.10.col_places, f32[9216,128]{1,0:T(8,128)} %get-tuple-element.11.front, f32[48,6,64,128]{3,2,1,0:T(8,128)} %get-tuple-element.12.children), custom_call_target="tpu_custom_call" | custom-call | tf_op jit(solution)/shard_map/pallas_call | solution.py:1011

commit v10 on v8

--- a/solution.py
+++ b/solution.py
@@ -167,8 +167,8 @@
 def kernel(
     child_map, child, root, out, bulk_in, row_out, col_out,
     marks, row_perms, col_places, chunk_buf, front, bulk_out, unit_in, front_out, front_in, cols, diag, rows, work,
-    pair, rows_f, rows_h, rows_l, prod, inv_h, inv_l, relay, kids, pick, wide_buf,
-    kids_s, keep_s, tab_s, s_marks, s_chunk, s_front, s_out, relay_s, relay_r, bulk_s, bulk_r, unit_s, unit_r, front_s, front_r,
+    pair, rows_f, rows_h, rows_l, prod, inv_h, inv_l, kids, pick, wide_buf,
+    kids_s, keep_s, tab_s, s_marks, s_chunk, s_front, s_out, bulk_s, bulk_r, unit_s, unit_r, front_s, front_r,
     cols_s, cols_r, hand_s, dz_s, dz_r, dy_s, dy_r, r1_s, r1_r, rz_s, rz_r, ry_s, ry_r,
 ):
     p = lax.axis_index("wide")
@@ -233,12 +233,8 @@
         greet(p, zl * 4 + mod(y + i, 4))
 
 
-    def greet_plane(i, carry):
-        greet(i, q_other)
-        return carry
-
-    lax.fori_loop(0, 16, greet_plane, 0)
-    pl.semaphore_wait(barrier, 34)
+    greet(p, q_other)
+    pl.semaphore_wait(barrier, 19)
 
     def packed(n, la, lb):
         base = mod(n, 4) * CHUNK
@@ -267,9 +263,6 @@
             front_out.at[m], front_in.at[slot], front_s.at[m], front_r.at[slot], owner, q
         )
 
-    zh = ph
-    xs = mod(chip, 4)
-
     def bulk_copy(k, dest):
         kk = 2 * k + core
         return remote(
@@ -280,43 +273,6 @@
     def keep_copy(k):
         return local(bulk_out.at[p * 3 + k], bulk_in.at[(2 * k + core) * 8 + chip], keep_s.at[k])
 
-    def first_copy(k, dest):
-        xd = mod(dest // 2, 4)
-        far = mod(xd - xs + 6, 4) == 0
-        xi = jnp.where(far, mod(xd + 1, 4), xd)
-        gap = mod(xs - xi + 4, 4)
-        way = jnp.where(far, 3, jnp.where(gap == 3, 2, gap))
-        zi = jnp.where(mod(core + xs + k, 2) == 0, zh, 1 - zh)
-        slot = k * 8 + way * 2 + core
-        return remote(
-            bulk_out.at[dest * 3 + k], relay.at[slot], bulk_s.at[dest * 3 + k],
-            relay_r.at[slot], (zi * 4 + xi) * 2 + mod(dest, 2), q_other,
-        )
-
-    def second_copy(k, way, cs):
-        slot = k * 8 + way * 2 + cs
-        side = jnp.where(jnp.logical_or(way == 1, way == 3), 1, jnp.where(way == 2, 3, 0))
-        source_x = mod(xs + side, 4)
-        dest_x = jnp.where(way == 3, mod(xs + 3, 4), xs)
-        source_z = jnp.where(mod(cs + source_x + k, 2) == 0, zh, 1 - zh)
-        dest = ((1 - source_z) * 4 + dest_x) * 2 + core
-        place = (2 * k + cs) * 8 + source_z * 4 + source_x
-        return dest, remote(
-            relay.at[slot], bulk_in.at[place], relay_s.at[slot], bulk_r.at[place], dest, q_other
-        )
-
-    def relay_one(i, carry):
-        k, way, cs = i // 8, mod(i, 8) // 2, mod(i, 2)
-        dest, copy = second_copy(k, way, cs)
-
-        @pl.when(jnp.logical_not(panel_row(2 * k + cs, dest)))
-        def _():
-            remote(
-                bulk_out.at[0], relay.at[i], bulk_s.at[0], relay_r.at[i], p, q_other
-            ).wait_recv()
-            copy.start()
-        return carry
-
     def panel_row(kk, dest):
         return jnp.logical_and(kk == 0, dest < 4)
 
@@ -354,13 +310,7 @@
 
         @pl.when(jnp.logical_not(panel_row(2 * k + core, dest)))
         def _():
-            crossing = dest // 8 != ph
-
-            @pl.when(crossing)
-            def _():
-                first_copy(k, dest).start()
-
-            @pl.when(jnp.logical_not(jnp.logical_or(crossing, dest == p)))
+            @pl.when(dest != p)
             def _():
                 bulk_copy(k, dest).start()
 
@@ -637,7 +587,6 @@
         rz.start()
 
     lax.fori_loop(20, 32, pack_fire, 0)
-    lax.fori_loop(0, 8, relay_one, 0)
 
     for i in range(1, 4):
         src = mod(y + i, 4)
@@ -649,7 +598,6 @@
     work[:, 0:SPAN] = 0.5 * (full + full.T)
     work[:, SPAN:] = jnp.zeros((SPAN, SPAN), F32)
 
-    lax.fori_loop(8, 16, relay_one, 0)
     factor_block(0, work, pair, Beside(32))
 
     @pl.when(jnp.logical_not(holder))
@@ -659,7 +607,6 @@
     for i in range(1, 4):
         ry(i).start()
 
-    lax.fori_loop(16, 24, relay_one, 0)
     factor_block(1, work, pair, Beside(40))
     factor_block(2, work, pair, None)
     factor_block(3, work, pair, Tables())
@@ -886,17 +833,6 @@
             return c
 
         lax.fori_loop(0, 6, one, 0)
-
-    def relayed(i, carry):
-        k, way, cs = i // 8, mod(i, 8) // 2, mod(i, 2)
-        dest, copy = second_copy(k, way, cs)
-
-        @pl.when(jnp.logical_not(panel_row(2 * k + cs, dest)))
-        def _():
-            copy.wait_send()
-        return carry
-
-    lax.fori_loop(0, 24, relayed, 0)
 
     def stored(kk, carry):
         store(kk).wait()
@@ -991,11 +927,10 @@
             vmem(768, 256),
             pltpu.VMEM((SPAN, SPAN), BF16),
             pltpu.VMEM((SPAN, SPAN), BF16),
-            vmem(24, 6, HALF, 128),
             vmem(CHILDREN, 6, HALF, 128),
             pltpu.VMEM((BLOCK, 1024), BF16),
             pltpu.VMEM((1024, 256), BF16),
-            sems(1), sems(3), sems(2), sems(1), sems(4), sems(1), sems(6), sems(24), sems(24), sems(48), sems(48), sems(24), sems(24),
+            sems(1), sems(3), sems(2), sems(1), sems(4), sems(1), sems(6), sems(48), sems(48), sems(24), sems(24),
             sems(6), sems(3), sems(24), sems(24), sems(24), sems(1), sems(1), sems(4), sems(4),
             sems(4), sems(1), sems(1), sems(1), sems(4), sems(4),
         ],

time: 202 us -> 220 us (1.089)
  the two profiles are of different devices: /device:TPU:85 before, /device:TPU:14 now
where the time goes in v10:
time: 220 us
  Pallas kernels  220 us (100%)
    pallas_call x1, Pallas kernels, body(): pl.pallas_call(kernel, out_shape=[jax.ShapeDtypeStruct(root.shape, F32),...  206 us
    pallas_call x1, Pallas kernels, body(): pl.pallas_call(add_children, grid=(ROW_BLOCKS,), out_shape=jax.ShapeDtype...  14 us

profile of v10, /device:TPU:14, one launch (start us, length us, event | category | flops | bytes accessed | tf_op | source)
XLA Modules:
  0.0 219.6 jit_solution(17435197744386273028)
XLA Ops:
  0.0 205.6 %shard_map.37 = (f32[9216,128]{1,0:T(8,128)}, f32[48,6,64,128]{3,2,1,0:T(8,128)}, s32[8,4,128]{2,1,0:T(4,128)}, s32[12,8,128]{2,1,0:T(8,128)}) custom-call(s32[8,6144]{1,0:T(8,128)} %child_map.1, f32[36864,64]{1,0:T(8,128)} %bitcast.3, f32[9216,128]{1,0:T(8,128)} %bitcast.4), custom_call_target="tpu_custom_call" | custom-call | tf_op jit(solution)/shard_map/pallas_call | solution.py:899
  205.6 14.0 %shard_map.38 = f32[9216,128]{1,0:T(8,128)} custom-call(s32[8,4,128]{2,1,0:T(4,128)} %get-tuple-element.9.row_perms, s32[12,8,128]{2,1,0:T(8,128)} %get-tuple-element.10.col_places, f32[9216,128]{1,0:T(8,128)} %get-tuple-element.11.front, f32[48,6,64,128]{3,2,1,0:T(8,128)} %get-tuple-element.12.children), custom_call_target="tpu_custom_call" | custom-call | tf_op jit(solution)/shard_map/pallas_call | solution.py:942

commit v11 on v7

--- a/solution.py
+++ b/solution.py
@@ -508,6 +508,9 @@
     first_slot = core
     last_slot = 1 + 2 * core
 
+    lax.fori_loop(0, 4, fire, 0)
+    lax.fori_loop(4, 8, pack_fire, 0)
+
     marks_load.wait()
     ranks = lax.broadcasted_iota(jnp.int32, (HALF, 128), 0)
     spots = lax.broadcasted_iota(jnp.int32, (HALF, 128), 1)
@@ -559,8 +562,6 @@
 
     lax.fori_loop(core, 1 + 2 * core, unit_table, 0)
     lax.fori_loop(first_slot, last_slot, own_unit, 0)
-    lax.fori_loop(0, 4, fire, 0)
-    lax.fori_loop(4, 8, pack_fire, 0)
     lax.fori_loop(first_slot, last_slot, spread_on, 0)
     lax.fori_loop(8, 10, pack_fire, 0)
 

time: 192 us -> 205 us (1.068)
  the two profiles are of different devices: /device:TPU:85 before, /device:TPU:20 now
where the time goes in v11:
time: 205 us; the launch traced here: 204 us
  Pallas kernels  204 us (100%)
    pallas_call x1, Pallas kernels, body(): pl.pallas_call(kernel, out_shape=[jax.ShapeDtypeStruct(root.shape, F32),...  190 us
    pallas_call x1, Pallas kernels, body(): pl.pallas_call(add_children, grid=(ROW_BLOCKS,), out_shape=jax.ShapeDtype...  14 us

profile of v11, /device:TPU:20, one launch (start us, length us, event | category | flops | bytes accessed | tf_op | source)
XLA Modules:
  0.0 204.3 jit_solution(6741895796202789932)
XLA Ops:
  0.0 190.3 %shard_map.37 = (f32[9216,128]{1,0:T(8,128)}, f32[48,6,64,128]{3,2,1,0:T(8,128)}, s32[8,4,128]{2,1,0:T(4,128)}, s32[12,8,128]{2,1,0:T(8,128)}) custom-call(s32[8,6144]{1,0:T(8,128)} %child_map.1, f32[36864,64]{1,0:T(8,128)} %bitcast.3, f32[9216,128]{1,0:T(8,128)} %bitcast.4), custom_call_target="tpu_custom_call" | custom-call | tf_op jit(solution)/shard_map/pallas_call | solution.py:964
  190.3 14.0 %shard_map.38 = f32[9216,128]{1,0:T(8,128)} custom-call(s32[8,4,128]{2,1,0:T(4,128)} %get-tuple-element.9.row_perms, s32[12,8,128]{2,1,0:T(8,128)} %get-tuple-element.10.col_places, f32[9216,128]{1,0:T(8,128)} %get-tuple-element.11.front, f32[48,6,64,128]{3,2,1,0:T(8,128)} %get-tuple-element.12.children), custom_call_target="tpu_custom_call" | custom-call | tf_op jit(solution)/shard_map/pallas_call | solution.py:1008
